TPU v7x, 256 devices: a whole 4x4x8 slice. The times are simulated.
256 devices in a mesh: pipe: 8 (over x, core), expert: 32 (over z, y).
Axes of the slice: x: 4, y: 4, z: 8, core: 2. Of those that a mesh axis runs over, the one named last changes fastest.
Arguments:
- inputs: bfloat16 [16, 256, 7168], P(None, 'expert'), may hold values from -6 to 6
- norm_gains: float32 [8, 7168], P('pipe'), may hold values from 0.25 to 1.75
- w_gate: bfloat16 [8, 7168, 4096], P('pipe', None, 'expert'), may hold values from -0.0625 to 0.0625
- w_up: bfloat16 [8, 7168, 4096], P('pipe', None, 'expert'), may hold values from -0.0625 to 0.0625
- w_down: bfloat16 [8, 4096, 7168], P('pipe', 'expert'), may hold values from -0.1875 to 0.1875
- expert_ids: int32 [8, 16, 256, 1], P('pipe', None, 'expert'), may hold values from 0 to 3; in each aligned block of 8 rows (0 to 7, 8 to 15, ..., all dimensions but the last counted through in order) at most 2 rows name the same one
- gate_weights: float32 [8, 16, 256], P('pipe', None, 'expert'), may hold values from 0.2 to 1.5
Outputs:
- states: bfloat16 [8, 16, 256, 7168], P('pipe', None, 'expert')
Inputs may be any that keep to these rules, and one draw needn't show every extreme that they name: `expert_ids`: of the tokens of one micro-batch on one device (aligned blocks of 8 tokens), exactly 2 are routed to each expert.
All inputs are finite; a program needn't handle non-finite values.
Results may differ from a plain program's by a relative error of at most 0.03.
Values may be sent and summed in bfloat16 or wider, within the bound.
A program may use at most 64 MiB of HBM per device.

v0:
```python
import jax
import jax.numpy as jnp
from jax import lax
from jax.sharding import PartitionSpec as P

GROUP = 8


def from_behind(value, axis, steps):
    count = lax.axis_size(axis)
    first, last = (max(0, -steps), min(count, count - steps))
    return lax.ppermute(value, axis, [(source, source + steps) for source in range(first, last)])


def expert_part(received, gate_cols, up_cols, down_rows):
    feature_width = received.shape[-1]
    flat = received.reshape(-1, feature_width)
    gate = jnp.dot(flat, gate_cols, preferred_element_type=jnp.float32)
    upper = jnp.dot(flat, up_cols, preferred_element_type=jnp.float32)
    hidden = (jax.nn.silu(gate) * upper).astype(jnp.bfloat16)
    part = jnp.dot(hidden, down_rows, preferred_element_type=jnp.float32).astype(jnp.bfloat16)
    return part.reshape(received.shape)


def local(inputs, norm_gains, w_gate, w_up, w_down, expert_ids, gate_weights):
    n_expert = lax.axis_size("expert")
    n_pipe = lax.axis_size("pipe")
    section_index = lax.axis_index("pipe")
    experts_here = n_expert // GROUP
    micro_count, row_count, feature_width = inputs.shape
    capacity = row_count // experts_here
    gains = norm_gains[0]
    gate_cols = w_gate[0]
    up_cols = w_up[0]
    down_rows = w_down[0]
    route_table = expert_ids[0, :, :, 0]
    weight_table = gate_weights[0]
    expert_range = jnp.arange(experts_here, dtype=jnp.int32)
    slot_range = jnp.arange(capacity, dtype=jnp.int32)

    def apply_layer(current, route_now, weight_now):
        current32 = current.astype(jnp.float32)
        scale = lax.rsqrt(jnp.mean(current32 * current32, axis=-1, keepdims=True) + 1e-06)
        normed = (current32 * scale * gains).astype(jnp.bfloat16)
        onehot = (route_now[:, None] == expert_range[None, :]).astype(jnp.int32)
        ranks = jnp.sum((jnp.cumsum(onehot, axis=0) - 1) * onehot, axis=1)
        select = (
            (route_now[None, None, :] == expert_range[:, None, None])
            & (ranks[None, None, :] == slot_range[None, :, None])
        ).astype(jnp.bfloat16)
        buffers = jnp.einsum(
            "ecr,rd->ecd", select, normed, preferred_element_type=jnp.float32
        ).astype(jnp.bfloat16)
        outgoing = jnp.repeat(buffers, GROUP, axis=0)
        part = expert_part(
            lax.all_to_all(outgoing, "expert", split_axis=0, concat_axis=0, tiled=True),
            gate_cols,
            up_cols,
            down_rows,
        )
        returned = lax.all_to_all(part, "expert", split_axis=0, concat_axis=0, tiled=True)
        summed = jnp.sum(
            returned.reshape(experts_here, GROUP, capacity, feature_width).astype(jnp.float32),
            axis=1,
        )
        combined = jnp.einsum(
            "ecr,ecd->rd", select.astype(jnp.float32), summed, precision=lax.Precision.HIGHEST
        )
        return (current32 + weight_now[:, None] * combined).astype(jnp.bfloat16)

    def step_fn(step_index, carry):
        incoming, states = carry
        micro_index = step_index - section_index
        is_valid = (micro_index >= 0) & (micro_index < micro_count)
        clipped = jnp.clip(micro_index, 0, micro_count - 1)
        fresh = lax.dynamic_index_in_dim(
            inputs, jnp.minimum(step_index, micro_count - 1), 0, keepdims=False
        )
        current = jnp.where(section_index == 0, fresh, incoming)
        route_now = lax.dynamic_index_in_dim(route_table, clipped, 0, keepdims=False)
        weight_now = lax.dynamic_index_in_dim(weight_table, clipped, 0, keepdims=False)
        result = apply_layer(current, route_now, weight_now)
        previous = lax.dynamic_index_in_dim(states, clipped, 0, keepdims=False)
        states = lax.dynamic_update_index_in_dim(
            states, jnp.where(is_valid, result, previous), clipped, 0
        )
        incoming = from_behind(result, "pipe", 1)
        return (incoming, states)

    start_states = jnp.zeros((micro_count, row_count, feature_width), jnp.bfloat16)
    start_incoming = jnp.zeros((row_count, feature_width), jnp.bfloat16)
    final_incoming, states = lax.fori_loop(
        0, micro_count + n_pipe - 1, step_fn, (start_incoming, start_states)
    )
    return states[None]


def solution(mesh):
    return jax.shard_map(
        local,
        mesh=mesh,
        in_specs=(
            P(None, "expert", None),
            P("pipe", None),
            P("pipe", None, "expert"),
            P("pipe", None, "expert"),
            P("pipe", "expert", None),
            P("pipe", None, "expert", None),
            P("pipe", None, "expert"),
        ),
        out_specs=P("pipe", None, "expert", None),
        check_vma=False,
    )
```

profile of v0, /device:TPU:1, one launch (start us, length us, event | category | flops | bytes accessed | tf_op | source)
XLA Modules:
  0.0 1712.7 jit_solution(780484589457785753)
XLA Ops:
  2.9 1709.7 %while.19 = (s32[]{:T(128)}, bf16[8,7168]{1,0:T(8,128)(2,1)S(1)}, bf16[16,8,7168]{2,1,0:T(8,128)(2,1)}, pred[]{:T(512)}, bf16[16,8,7168]{2,1,0:T(8,128)(2,1)}, /...) while((s32[]{:T(128)}, bf16[8,7168]{1,0:T(8,128)(2,1)S(1)}, ...), condition=%wide.region_5.6_spmd.clone.clone, body=%wide.region_0.5_spmd.clone.clone.sunk | while | flops 360915552 | bytes 20968876 | solution.py:92
  5.1 35.3 %all_to_all.30 = bf16[32,2,7168]{2,1,0:T(2,128)(2,1)S(1)} all-to-all(bf16[32,2,7168]{2,1,0:T(2,128)(2,1)S(1)} %bitcast.66), channel_id=1, replica_groups=mesh['pipe'=8,'expert'=32] {'expert'}, dimensions={0} | all-to-all | bytes 1835008 | tf_op jit(solution)/shard_map/while/body/eval_jaxpr/all_to_all | solution.py:56
  54.0 21.7 %all-to-all-done.1 = bf16[32,2,7168]{2,1,0:T(2,128)(2,1)S(1)} async-done(((bf16[32,2,7168]{2,1,0:T(2,128)(2,1)}), bf16[32,2,7168]{2,1,0:T(2,128)(2,1)S(1)}, u32[]{:S(2)}, u32[]{:S(2)}) %all-to-all-start.1) | async-done | bytes 917536 | tf_op jit(solution)/shard_map/while/body/eval_jaxpr/all_to_all | solution.py:61
  77.5 6.6 collective-permute-start
  88.1 28.9 %all_to_all.30 = bf16[32,2,7168]{2,1,0:T(2,128)(2,1)S(1)} all-to-all(bf16[32,2,7168]{2,1,0:T(2,128)(2,1)S(1)} %bitcast.66), channel_id=1, replica_groups=mesh['pipe'=8,'expert'=32] {'expert'}, dimensions={0} | all-to-all | bytes 1835008 | tf_op jit(solution)/shard_map/while/body/eval_jaxpr/all_to_all | solution.py:56
  129.5 23.8 %all-to-all-done.1 = bf16[32,2,7168]{2,1,0:T(2,128)(2,1)S(1)} async-done(((bf16[32,2,7168]{2,1,0:T(2,128)(2,1)}), bf16[32,2,7168]{2,1,0:T(2,128)(2,1)S(1)}, u32[]{:S(2)}, u32[]{:S(2)}) %all-to-all-start.1) | async-done | bytes 917536 | tf_op jit(solution)/shard_map/while/body/eval_jaxpr/all_to_all | solution.py:61
  164.3 28.3 %all_to_all.30 = bf16[32,2,7168]{2,1,0:T(2,128)(2,1)S(1)} all-to-all(bf16[32,2,7168]{2,1,0:T(2,128)(2,1)S(1)} %bitcast.66), channel_id=1, replica_groups=mesh['pipe'=8,'expert'=32] {'expert'}, dimensions={0} | all-to-all | bytes 1835008 | tf_op jit(solution)/shard_map/while/body/eval_jaxpr/all_to_all | solution.py:56
  205.2 24.6 %all-to-all-done.1 = bf16[32,2,7168]{2,1,0:T(2,128)(2,1)S(1)} async-done(((bf16[32,2,7168]{2,1,0:T(2,128)(2,1)}), bf16[32,2,7168]{2,1,0:T(2,128)(2,1)S(1)}, u32[]{:S(2)}, u32[]{:S(2)}) %all-to-all-start.1) | async-done | bytes 917536 | tf_op jit(solution)/shard_map/while/body/eval_jaxpr/all_to_all | solution.py:61
  240.3 28.1 %all_to_all.30 = bf16[32,2,7168]{2,1,0:T(2,128)(2,1)S(1)} all-to-all(bf16[32,2,7168]{2,1,0:T(2,128)(2,1)S(1)} %bitcast.66), channel_id=1, replica_groups=mesh['pipe'=8,'expert'=32] {'expert'}, dimensions={0} | all-to-all | bytes 1835008 | tf_op jit(solution)/shard_map/while/body/eval_jaxpr/all_to_all | solution.py:56
  280.9 23.8 %all-to-all-done.1 = bf16[32,2,7168]{2,1,0:T(2,128)(2,1)S(1)} async-done(((bf16[32,2,7168]{2,1,0:T(2,128)(2,1)}), bf16[32,2,7168]{2,1,0:T(2,128)(2,1)S(1)}, u32[]{:S(2)}, u32[]{:S(2)}) %all-to-all-start.1) | async-done | bytes 917536 | tf_op jit(solution)/shard_map/while/body/eval_jaxpr/all_to_all | solution.py:61
  312.4 30.2 %all_to_all.30 = bf16[32,2,7168]{2,1,0:T(2,128)(2,1)S(1)} all-to-all(bf16[32,2,7168]{2,1,0:T(2,128)(2,1)S(1)} %bitcast.66), channel_id=1, replica_groups=mesh['pipe'=8,'expert'=32] {'expert'}, dimensions={0} | all-to-all | bytes 1835008 | tf_op jit(solution)/shard_map/while/body/eval_jaxpr/all_to_all | solution.py:56
  355.8 22.3 %all-to-all-done.1 = bf16[32,2,7168]{2,1,0:T(2,128)(2,1)S(1)} async-done(((bf16[32,2,7168]{2,1,0:T(2,128)(2,1)}), bf16[32,2,7168]{2,1,0:T(2,128)(2,1)S(1)}, u32[]{:S(2)}, u32[]{:S(2)}) %all-to-all-start.1) | async-done | bytes 917536 | tf_op jit(solution)/shard_map/while/body/eval_jaxpr/all_to_all | solution.py:61
  387.3 29.3 %all_to_all.30 = bf16[32,2,7168]{2,1,0:T(2,128)(2,1)S(1)} all-to-all(bf16[32,2,7168]{2,1,0:T(2,128)(2,1)S(1)} %bitcast.66), channel_id=1, replica_groups=mesh['pipe'=8,'expert'=32] {'expert'}, dimensions={0} | all-to-all | bytes 1835008 | tf_op jit(solution)/shard_map/while/body/eval_jaxpr/all_to_all | solution.py:56
  429.5 22.0 %all-to-all-done.1 = bf16[32,2,7168]{2,1,0:T(2,128)(2,1)S(1)} async-done(((bf16[32,2,7168]{2,1,0:T(2,128)(2,1)}), bf16[32,2,7168]{2,1,0:T(2,128)(2,1)S(1)}, u32[]{:S(2)}, u32[]{:S(2)}) %all-to-all-start.1) | async-done | bytes 917536 | tf_op jit(solution)/shard_map/while/body/eval_jaxpr/all_to_all | solution.py:61
  460.9 29.4 %all_to_all.30 = bf16[32,2,7168]{2,1,0:T(2,128)(2,1)S(1)} all-to-all(bf16[32,2,7168]{2,1,0:T(2,128)(2,1)S(1)} %bitcast.66), channel_id=1, replica_groups=mesh['pipe'=8,'expert'=32] {'expert'}, dimensions={0} | all-to-all | bytes 1835008 | tf_op jit(solution)/shard_map/while/body/eval_jaxpr/all_to_all | solution.py:56
  503.3 22.0 %all-to-all-done.1 = bf16[32,2,7168]{2,1,0:T(2,128)(2,1)S(1)} async-done(((bf16[32,2,7168]{2,1,0:T(2,128)(2,1)}), bf16[32,2,7168]{2,1,0:T(2,128)(2,1)S(1)}, u32[]{:S(2)}, u32[]{:S(2)}) %all-to-all-start.1) | async-done | bytes 917536 | tf_op jit(solution)/shard_map/while/body/eval_jaxpr/all_to_all | solution.py:61
  534.7 29.4 %all_to_all.30 = bf16[32,2,7168]{2,1,0:T(2,128)(2,1)S(1)} all-to-all(bf16[32,2,7168]{2,1,0:T(2,128)(2,1)S(1)} %bitcast.66), channel_id=1, replica_groups=mesh['pipe'=8,'expert'=32] {'expert'}, dimensions={0} | all-to-all | bytes 1835008 | tf_op jit(solution)/shard_map/while/body/eval_jaxpr/all_to_all | solution.py:56
  577.1 22.0 %all-to-all-done.1 = bf16[32,2,7168]{2,1,0:T(2,128)(2,1)S(1)} async-done(((bf16[32,2,7168]{2,1,0:T(2,128)(2,1)}), bf16[32,2,7168]{2,1,0:T(2,128)(2,1)S(1)}, u32[]{:S(2)}, u32[]{:S(2)}) %all-to-all-start.1) | async-done | bytes 917536 | tf_op jit(solution)/shard_map/while/body/eval_jaxpr/all_to_all | solution.py:61
  608.5 29.4 %all_to_all.30 = bf16[32,2,7168]{2,1,0:T(2,128)(2,1)S(1)} all-to-all(bf16[32,2,7168]{2,1,0:T(2,128)(2,1)S(1)} %bitcast.66), channel_id=1, replica_groups=mesh['pipe'=8,'expert'=32] {'expert'}, dimensions={0} | all-to-all | bytes 1835008 | tf_op jit(solution)/shard_map/while/body/eval_jaxpr/all_to_all | solution.py:56
  650.8 22.0 %all-to-all-done.1 = bf16[32,2,7168]{2,1,0:T(2,128)(2,1)S(1)} async-done(((bf16[32,2,7168]{2,1,0:T(2,128)(2,1)}), bf16[32,2,7168]{2,1,0:T(2,128)(2,1)S(1)}, u32[]{:S(2)}, u32[]{:S(2)}) %all-to-all-start.1) | async-done | bytes 917536 | tf_op jit(solution)/shard_map/while/body/eval_jaxpr/all_to_all | solution.py:61
  682.2 29.4 %all_to_all.30 = bf16[32,2,7168]{2,1,0:T(2,128)(2,1)S(1)} all-to-all(bf16[32,2,7168]{2,1,0:T(2,128)(2,1)S(1)} %bitcast.66), channel_id=1, replica_groups=mesh['pipe'=8,'expert'=32] {'expert'}, dimensions={0} | all-to-all | bytes 1835008 | tf_op jit(solution)/shard_map/while/body/eval_jaxpr/all_to_all | solution.py:56
  724.6 22.0 %all-to-all-done.1 = bf16[32,2,7168]{2,1,0:T(2,128)(2,1)S(1)} async-done(((bf16[32,2,7168]{2,1,0:T(2,128)(2,1)}), bf16[32,2,7168]{2,1,0:T(2,128)(2,1)S(1)}, u32[]{:S(2)}, u32[]{:S(2)}) %all-to-all-start.1) | async-done | bytes 917536 | tf_op jit(solution)/shard_map/while/body/eval_jaxpr/all_to_all | solution.py:61
  756.0 29.4 %all_to_all.30 = bf16[32,2,7168]{2,1,0:T(2,128)(2,1)S(1)} all-to-all(bf16[32,2,7168]{2,1,0:T(2,128)(2,1)S(1)} %bitcast.66), channel_id=1, replica_groups=mesh['pipe'=8,'expert'=32] {'expert'}, dimensions={0} | all-to-all | bytes 1835008 | tf_op jit(solution)/shard_map/while/body/eval_jaxpr/all_to_all | solution.py:56
  798.3 22.0 %all-to-all-done.1 = bf16[32,2,7168]{2,1,0:T(2,128)(2,1)S(1)} async-done(((bf16[32,2,7168]{2,1,0:T(2,128)(2,1)}), bf16[32,2,7168]{2,1,0:T(2,128)(2,1)S(1)}, u32[]{:S(2)}, u32[]{:S(2)}) %all-to-all-start.1) | async-done | bytes 917536 | tf_op jit(solution)/shard_map/while/body/eval_jaxpr/all_to_all | solution.py:61
  829.7 29.4 %all_to_all.30 = bf16[32,2,7168]{2,1,0:T(2,128)(2,1)S(1)} all-to-all(bf16[32,2,7168]{2,1,0:T(2,128)(2,1)S(1)} %bitcast.66), channel_id=1, replica_groups=mesh['pipe'=8,'expert'=32] {'expert'}, dimensions={0} | all-to-all | bytes 1835008 | tf_op jit(solution)/shard_map/while/body/eval_jaxpr/all_to_all | solution.py:56
  872.1 22.0 %all-to-all-done.1 = bf16[32,2,7168]{2,1,0:T(2,128)(2,1)S(1)} async-done(((bf16[32,2,7168]{2,1,0:T(2,128)(2,1)}), bf16[32,2,7168]{2,1,0:T(2,128)(2,1)S(1)}, u32[]{:S(2)}, u32[]{:S(2)}) %all-to-all-start.1) | async-done | bytes 917536 | tf_op jit(solution)/shard_map/while/body/eval_jaxpr/all_to_all | solution.py:61
  903.5 29.4 %all_to_all.30 = bf16[32,2,7168]{2,1,0:T(2,128)(2,1)S(1)} all-to-all(bf16[32,2,7168]{2,1,0:T(2,128)(2,1)S(1)} %bitcast.66), channel_id=1, replica_groups=mesh['pipe'=8,'expert'=32] {'expert'}, dimensions={0} | all-to-all | bytes 1835008 | tf_op jit(solution)/shard_map/while/body/eval_jaxpr/all_to_all | solution.py:56
  945.9 22.0 %all-to-all-done.1 = bf16[32,2,7168]{2,1,0:T(2,128)(2,1)S(1)} async-done(((bf16[32,2,7168]{2,1,0:T(2,128)(2,1)}), bf16[32,2,7168]{2,1,0:T(2,128)(2,1)S(1)}, u32[]{:S(2)}, u32[]{:S(2)}) %all-to-all-start.1) | async-done | bytes 917536 | tf_op jit(solution)/shard_map/while/body/eval_jaxpr/all_to_all | solution.py:61
  977.3 29.4 %all_to_all.30 = bf16[32,2,7168]{2,1,0:T(2,128)(2,1)S(1)} all-to-all(bf16[32,2,7168]{2,1,0:T(2,128)(2,1)S(1)} %bitcast.66), channel_id=1, replica_groups=mesh['pipe'=8,'expert'=32] {'expert'}, dimensions={0} | all-to-all | bytes 1835008 | tf_op jit(solution)/shard_map/while/body/eval_jaxpr/all_to_all | solution.py:56
  1019.6 22.0 %all-to-all-done.1 = bf16[32,2,7168]{2,1,0:T(2,128)(2,1)S(1)} async-done(((bf16[32,2,7168]{2,1,0:T(2,128)(2,1)}), bf16[32,2,7168]{2,1,0:T(2,128)(2,1)S(1)}, u32[]{:S(2)}, u32[]{:S(2)}) %all-to-all-start.1) | async-done | bytes 917536 | tf_op jit(solution)/shard_map/while/body/eval_jaxpr/all_to_all | solution.py:61
  1051.0 29.4 %all_to_all.30 = bf16[32,2,7168]{2,1,0:T(2,128)(2,1)S(1)} all-to-all(bf16[32,2,7168]{2,1,0:T(2,128)(2,1)S(1)} %bitcast.66), channel_id=1, replica_groups=mesh['pipe'=8,'expert'=32] {'expert'}, dimensions={0} | all-to-all | bytes 1835008 | tf_op jit(solution)/shard_map/while/body/eval_jaxpr/all_to_all | solution.py:56
  1093.4 22.0 %all-to-all-done.1 = bf16[32,2,7168]{2,1,0:T(2,128)(2,1)S(1)} async-done(((bf16[32,2,7168]{2,1,0:T(2,128)(2,1)}), bf16[32,2,7168]{2,1,0:T(2,128)(2,1)S(1)}, u32[]{:S(2)}, u32[]{:S(2)}) %all-to-all-start.1) | async-done | bytes 917536 | tf_op jit(solution)/shard_map/while/body/eval_jaxpr/all_to_all | solution.py:61
  1124.8 29.4 %all_to_all.30 = bf16[32,2,7168]{2,1,0:T(2,128)(2,1)S(1)} all-to-all(bf16[32,2,7168]{2,1,0:T(2,128)(2,1)S(1)} %bitcast.66), channel_id=1, replica_groups=mesh['pipe'=8,'expert'=32] {'expert'}, dimensions={0} | all-to-all | bytes 1835008 | tf_op jit(solution)/shard_map/while/body/eval_jaxpr/all_to_all | solution.py:56
  1167.1 22.0 %all-to-all-done.1 = bf16[32,2,7168]{2,1,0:T(2,128)(2,1)S(1)} async-done(((bf16[32,2,7168]{2,1,0:T(2,128)(2,1)}), bf16[32,2,7168]{2,1,0:T(2,128)(2,1)S(1)}, u32[]{:S(2)}, u32[]{:S(2)}) %all-to-all-start.1) | async-done | bytes 917536 | tf_op jit(solution)/shard_map/while/body/eval_jaxpr/all_to_all | solution.py:61
  1198.5 29.4 %all_to_all.30 = bf16[32,2,7168]{2,1,0:T(2,128)(2,1)S(1)} all-to-all(bf16[32,2,7168]{2,1,0:T(2,128)(2,1)S(1)} %bitcast.66), channel_id=1, replica_groups=mesh['pipe'=8,'expert'=32] {'expert'}, dimensions={0} | all-to-all | bytes 1835008 | tf_op jit(solution)/shard_map/while/body/eval_jaxpr/all_to_all | solution.py:56
  1240.9 22.0 %all-to-all-done.1 = bf16[32,2,7168]{2,1,0:T(2,128)(2,1)S(1)} async-done(((bf16[32,2,7168]{2,1,0:T(2,128)(2,1)}), bf16[32,2,7168]{2,1,0:T(2,128)(2,1)S(1)}, u32[]{:S(2)}, u32[]{:S(2)}) %all-to-all-start.1) | async-done | bytes 917536 | tf_op jit(solution)/shard_map/while/body/eval_jaxpr/all_to_all | solution.py:61
  1272.3 29.4 %all_to_all.30 = bf16[32,2,7168]{2,1,0:T(2,128)(2,1)S(1)} all-to-all(bf16[32,2,7168]{2,1,0:T(2,128)(2,1)S(1)} %bitcast.66), channel_id=1, replica_groups=mesh['pipe'=8,'expert'=32] {'expert'}, dimensions={0} | all-to-all | bytes 1835008 | tf_op jit(solution)/shard_map/while/body/eval_jaxpr/all_to_all | solution.py:56
  1314.7 22.0 %all-to-all-done.1 = bf16[32,2,7168]{2,1,0:T(2,128)(2,1)S(1)} async-done(((bf16[32,2,7168]{2,1,0:T(2,128)(2,1)}), bf16[32,2,7168]{2,1,0:T(2,128)(2,1)S(1)}, u32[]{:S(2)}, u32[]{:S(2)}) %all-to-all-start.1) | async-done | bytes 917536 | tf_op jit(solution)/shard_map/while/body/eval_jaxpr/all_to_all | solution.py:61
  1346.1 29.4 %all_to_all.30 = bf16[32,2,7168]{2,1,0:T(2,128)(2,1)S(1)} all-to-all(bf16[32,2,7168]{2,1,0:T(2,128)(2,1)S(1)} %bitcast.66), channel_id=1, replica_groups=mesh['pipe'=8,'expert'=32] {'expert'}, dimensions={0} | all-to-all | bytes 1835008 | tf_op jit(solution)/shard_map/while/body/eval_jaxpr/all_to_all | solution.py:56
  1388.4 22.0 %all-to-all-done.1 = bf16[32,2,7168]{2,1,0:T(2,128)(2,1)S(1)} async-done(((bf16[32,2,7168]{2,1,0:T(2,128)(2,1)}), bf16[32,2,7168]{2,1,0:T(2,128)(2,1)S(1)}, u32[]{:S(2)}, u32[]{:S(2)}) %all-to-all-start.1) | async-done | bytes 917536 | tf_op jit(solution)/shard_map/while/body/eval_jaxpr/all_to_all | solution.py:61
  1419.8 29.4 %all_to_all.30 = bf16[32,2,7168]{2,1,0:T(2,128)(2,1)S(1)} all-to-all(bf16[32,2,7168]{2,1,0:T(2,128)(2,1)S(1)} %bitcast.66), channel_id=1, replica_groups=mesh['pipe'=8,'expert'=32] {'expert'}, dimensions={0} | all-to-all | bytes 1835008 | tf_op jit(solution)/shard_map/while/body/eval_jaxpr/all_to_all | solution.py:56
  1462.2 22.0 %all-to-all-done.1 = bf16[32,2,7168]{2,1,0:T(2,128)(2,1)S(1)} async-done(((bf16[32,2,7168]{2,1,0:T(2,128)(2,1)}), bf16[32,2,7168]{2,1,0:T(2,128)(2,1)S(1)}, u32[]{:S(2)}, u32[]{:S(2)}) %all-to-all-start.1) | async-done | bytes 917536 | tf_op jit(solution)/shard_map/while/body/eval_jaxpr/all_to_all | solution.py:61
  1493.6 29.4 %all_to_all.30 = bf16[32,2,7168]{2,1,0:T(2,128)(2,1)S(1)} all-to-all(bf16[32,2,7168]{2,1,0:T(2,128)(2,1)S(1)} %bitcast.66), channel_id=1, replica_groups=mesh['pipe'=8,'expert'=32] {'expert'}, dimensions={0} | all-to-all | bytes 1835008 | tf_op jit(solution)/shard_map/while/body/eval_jaxpr/all_to_all | solution.py:56
  1535.9 22.0 %all-to-all-done.1 = bf16[32,2,7168]{2,1,0:T(2,128)(2,1)S(1)} async-done(((bf16[32,2,7168]{2,1,0:T(2,128)(2,1)}), bf16[32,2,7168]{2,1,0:T(2,128)(2,1)S(1)}, u32[]{:S(2)}, u32[]{:S(2)}) %all-to-all-start.1) | async-done | bytes 917536 | tf_op jit(solution)/shard_map/while/body/eval_jaxpr/all_to_all | solution.py:61
  1567.3 29.4 %all_to_all.30 = bf16[32,2,7168]{2,1,0:T(2,128)(2,1)S(1)} all-to-all(bf16[32,2,7168]{2,1,0:T(2,128)(2,1)S(1)} %bitcast.66), channel_id=1, replica_groups=mesh['pipe'=8,'expert'=32] {'expert'}, dimensions={0} | all-to-all | bytes 1835008 | tf_op jit(solution)/shard_map/while/body/eval_jaxpr/all_to_all | solution.py:56
  1609.7 22.0 %all-to-all-done.1 = bf16[32,2,7168]{2,1,0:T(2,128)(2,1)S(1)} async-done(((bf16[32,2,7168]{2,1,0:T(2,128)(2,1)}), bf16[32,2,7168]{2,1,0:T(2,128)(2,1)S(1)}, u32[]{:S(2)}, u32[]{:S(2)}) %all-to-all-start.1) | async-done | bytes 917536 | tf_op jit(solution)/shard_map/while/body/eval_jaxpr/all_to_all | solution.py:61
  1641.1 29.4 %all_to_all.30 = bf16[32,2,7168]{2,1,0:T(2,128)(2,1)S(1)} all-to-all(bf16[32,2,7168]{2,1,0:T(2,128)(2,1)S(1)} %bitcast.66), channel_id=1, replica_groups=mesh['pipe'=8,'expert'=32] {'expert'}, dimensions={0} | all-to-all | bytes 1835008 | tf_op jit(solution)/shard_map/while/body/eval_jaxpr/all_to_all | solution.py:56
  1683.5 22.0 %all-to-all-done.1 = bf16[32,2,7168]{2,1,0:T(2,128)(2,1)S(1)} async-done(((bf16[32,2,7168]{2,1,0:T(2,128)(2,1)}), bf16[32,2,7168]{2,1,0:T(2,128)(2,1)S(1)}, u32[]{:S(2)}, u32[]{:S(2)}) %all-to-all-start.1) | async-done | bytes 917536 | tf_op jit(solution)/shard_map/while/body/eval_jaxpr/all_to_all | solution.py:61
  (511 shorter events, 511.2 us)
Async XLA Ops:
  0.0 2.9 copy-start
  46.9 28.8 %all-to-all-start.1 = ((bf16[32,2,7168]{2,1,0:T(2,128)(2,1)}), bf16[32,2,7168]{2,1,0:T(2,128)(2,1)S(1)}, u32[]{:S(2)}, u32[]{:S(2)}) async-start(bf16[32,2,7168]{2,1,0:T(2,128)(2,1)} %reshape.139), calls=%async_computation.1 | async-start | bytes 1835008 | tf_op jit(solution)/shard_map/while/body/eval_jaxpr/all_to_all | solution.py:61
  77.5 8.4 collective-permute-start
  123.5 29.8 %all-to-all-start.1 = ((bf16[32,2,7168]{2,1,0:T(2,128)(2,1)}), bf16[32,2,7168]{2,1,0:T(2,128)(2,1)S(1)}, u32[]{:S(2)}, u32[]{:S(2)}) async-start(bf16[32,2,7168]{2,1,0:T(2,128)(2,1)} %reshape.139), calls=%async_computation.1 | async-start | bytes 1835008 | tf_op jit(solution)/shard_map/while/body/eval_jaxpr/all_to_all | solution.py:61
  155.2 6.9 collective-permute-start
  199.0 30.8 %all-to-all-start.1 = ((bf16[32,2,7168]{2,1,0:T(2,128)(2,1)}), bf16[32,2,7168]{2,1,0:T(2,128)(2,1)S(1)}, u32[]{:S(2)}, u32[]{:S(2)}) async-start(bf16[32,2,7168]{2,1,0:T(2,128)(2,1)} %reshape.139), calls=%async_computation.1 | async-start | bytes 1835008 | tf_op jit(solution)/shard_map/while/body/eval_jaxpr/all_to_all | solution.py:61
  231.6 6.5 collective-permute-start
  274.8 29.9 %all-to-all-start.1 = ((bf16[32,2,7168]{2,1,0:T(2,128)(2,1)}), bf16[32,2,7168]{2,1,0:T(2,128)(2,1)S(1)}, u32[]{:S(2)}, u32[]{:S(2)}) async-start(bf16[32,2,7168]{2,1,0:T(2,128)(2,1)} %reshape.139), calls=%async_computation.1 | async-start | bytes 1835008 | tf_op jit(solution)/shard_map/while/body/eval_jaxpr/all_to_all | solution.py:61
  306.6 3.7 collective-permute-start
  349.1 29.0 %all-to-all-start.1 = ((bf16[32,2,7168]{2,1,0:T(2,128)(2,1)}), bf16[32,2,7168]{2,1,0:T(2,128)(2,1)S(1)}, u32[]{:S(2)}, u32[]{:S(2)}) async-start(bf16[32,2,7168]{2,1,0:T(2,128)(2,1)} %reshape.139), calls=%async_computation.1 | async-start | bytes 1835008 | tf_op jit(solution)/shard_map/while/body/eval_jaxpr/all_to_all | solution.py:61
  379.9 5.3 collective-permute-start
  423.1 28.5 %all-to-all-start.1 = ((bf16[32,2,7168]{2,1,0:T(2,128)(2,1)}), bf16[32,2,7168]{2,1,0:T(2,128)(2,1)S(1)}, u32[]{:S(2)}, u32[]{:S(2)}) async-start(bf16[32,2,7168]{2,1,0:T(2,128)(2,1)} %reshape.139), calls=%async_computation.1 | async-start | bytes 1835008 | tf_op jit(solution)/shard_map/while/body/eval_jaxpr/all_to_all | solution.py:61
  453.4 5.4 collective-permute-start
  496.8 28.5 %all-to-all-start.1 = ((bf16[32,2,7168]{2,1,0:T(2,128)(2,1)}), bf16[32,2,7168]{2,1,0:T(2,128)(2,1)S(1)}, u32[]{:S(2)}, u32[]{:S(2)}) async-start(bf16[32,2,7168]{2,1,0:T(2,128)(2,1)} %reshape.139), calls=%async_computation.1 | async-start | bytes 1835008 | tf_op jit(solution)/shard_map/while/body/eval_jaxpr/all_to_all | solution.py:61
  527.2 5.4 collective-permute-start
  570.6 28.5 %all-to-all-start.1 = ((bf16[32,2,7168]{2,1,0:T(2,128)(2,1)}), bf16[32,2,7168]{2,1,0:T(2,128)(2,1)S(1)}, u32[]{:S(2)}, u32[]{:S(2)}) async-start(bf16[32,2,7168]{2,1,0:T(2,128)(2,1)} %reshape.139), calls=%async_computation.1 | async-start | bytes 1835008 | tf_op jit(solution)/shard_map/while/body/eval_jaxpr/all_to_all | solution.py:61
  600.9 5.4 collective-permute-start
  644.4 28.5 %all-to-all-start.1 = ((bf16[32,2,7168]{2,1,0:T(2,128)(2,1)}), bf16[32,2,7168]{2,1,0:T(2,128)(2,1)S(1)}, u32[]{:S(2)}, u32[]{:S(2)}) async-start(bf16[32,2,7168]{2,1,0:T(2,128)(2,1)} %reshape.139), calls=%async_computation.1 | async-start | bytes 1835008 | tf_op jit(solution)/shard_map/while/body/eval_jaxpr/all_to_all | solution.py:61
  674.7 5.4 collective-permute-start
  718.1 28.5 %all-to-all-start.1 = ((bf16[32,2,7168]{2,1,0:T(2,128)(2,1)}), bf16[32,2,7168]{2,1,0:T(2,128)(2,1)S(1)}, u32[]{:S(2)}, u32[]{:S(2)}) async-start(bf16[32,2,7168]{2,1,0:T(2,128)(2,1)} %reshape.139), calls=%async_computation.1 | async-start | bytes 1835008 | tf_op jit(solution)/shard_map/while/body/eval_jaxpr/all_to_all | solution.py:61
  748.5 5.4 collective-permute-start
  791.9 28.5 %all-to-all-start.1 = ((bf16[32,2,7168]{2,1,0:T(2,128)(2,1)}), bf16[32,2,7168]{2,1,0:T(2,128)(2,1)S(1)}, u32[]{:S(2)}, u32[]{:S(2)}) async-start(bf16[32,2,7168]{2,1,0:T(2,128)(2,1)} %reshape.139), calls=%async_computation.1 | async-start | bytes 1835008 | tf_op jit(solution)/shard_map/while/body/eval_jaxpr/all_to_all | solution.py:61
  822.2 5.4 collective-permute-start
  865.6 28.5 %all-to-all-start.1 = ((bf16[32,2,7168]{2,1,0:T(2,128)(2,1)}), bf16[32,2,7168]{2,1,0:T(2,128)(2,1)S(1)}, u32[]{:S(2)}, u32[]{:S(2)}) async-start(bf16[32,2,7168]{2,1,0:T(2,128)(2,1)} %reshape.139), calls=%async_computation.1 | async-start | bytes 1835008 | tf_op jit(solution)/shard_map/while/body/eval_jaxpr/all_to_all | solution.py:61
  896.0 5.4 collective-permute-start
  939.4 28.5 %all-to-all-start.1 = ((bf16[32,2,7168]{2,1,0:T(2,128)(2,1)}), bf16[32,2,7168]{2,1,0:T(2,128)(2,1)S(1)}, u32[]{:S(2)}, u32[]{:S(2)}) async-start(bf16[32,2,7168]{2,1,0:T(2,128)(2,1)} %reshape.139), calls=%async_computation.1 | async-start | bytes 1835008 | tf_op jit(solution)/shard_map/while/body/eval_jaxpr/all_to_all | solution.py:61
  969.7 5.4 collective-permute-start
  1013.1 28.5 %all-to-all-start.1 = ((bf16[32,2,7168]{2,1,0:T(2,128)(2,1)}), bf16[32,2,7168]{2,1,0:T(2,128)(2,1)S(1)}, u32[]{:S(2)}, u32[]{:S(2)}) async-start(bf16[32,2,7168]{2,1,0:T(2,128)(2,1)} %reshape.139), calls=%async_computation.1 | async-start | bytes 1835008 | tf_op jit(solution)/shard_map/while/body/eval_jaxpr/all_to_all | solution.py:61
  1043.5 5.4 collective-permute-start
  1086.9 28.5 %all-to-all-start.1 = ((bf16[32,2,7168]{2,1,0:T(2,128)(2,1)}), bf16[32,2,7168]{2,1,0:T(2,128)(2,1)S(1)}, u32[]{:S(2)}, u32[]{:S(2)}) async-start(bf16[32,2,7168]{2,1,0:T(2,128)(2,1)} %reshape.139), calls=%async_computation.1 | async-start | bytes 1835008 | tf_op jit(solution)/shard_map/while/body/eval_jaxpr/all_to_all | solution.py:61
  1117.2 5.4 collective-permute-start
  1160.7 28.5 %all-to-all-start.1 = ((bf16[32,2,7168]{2,1,0:T(2,128)(2,1)}), bf16[32,2,7168]{2,1,0:T(2,128)(2,1)S(1)}, u32[]{:S(2)}, u32[]{:S(2)}) async-start(bf16[32,2,7168]{2,1,0:T(2,128)(2,1)} %reshape.139), calls=%async_computation.1 | async-start | bytes 1835008 | tf_op jit(solution)/shard_map/while/body/eval_jaxpr/all_to_all | solution.py:61
  1191.0 5.4 collective-permute-start
  1234.4 28.5 %all-to-all-start.1 = ((bf16[32,2,7168]{2,1,0:T(2,128)(2,1)}), bf16[32,2,7168]{2,1,0:T(2,128)(2,1)S(1)}, u32[]{:S(2)}, u32[]{:S(2)}) async-start(bf16[32,2,7168]{2,1,0:T(2,128)(2,1)} %reshape.139), calls=%async_computation.1 | async-start | bytes 1835008 | tf_op jit(solution)/shard_map/while/body/eval_jaxpr/all_to_all | solution.py:61
  1264.8 5.4 collective-permute-start
  1308.2 28.5 %all-to-all-start.1 = ((bf16[32,2,7168]{2,1,0:T(2,128)(2,1)}), bf16[32,2,7168]{2,1,0:T(2,128)(2,1)S(1)}, u32[]{:S(2)}, u32[]{:S(2)}) async-start(bf16[32,2,7168]{2,1,0:T(2,128)(2,1)} %reshape.139), calls=%async_computation.1 | async-start | bytes 1835008 | tf_op jit(solution)/shard_map/while/body/eval_jaxpr/all_to_all | solution.py:61
  1338.5 5.4 collective-permute-start
  1382.0 28.5 %all-to-all-start.1 = ((bf16[32,2,7168]{2,1,0:T(2,128)(2,1)}), bf16[32,2,7168]{2,1,0:T(2,128)(2,1)S(1)}, u32[]{:S(2)}, u32[]{:S(2)}) async-start(bf16[32,2,7168]{2,1,0:T(2,128)(2,1)} %reshape.139), calls=%async_computation.1 | async-start | bytes 1835008 | tf_op jit(solution)/shard_map/while/body/eval_jaxpr/all_to_all | solution.py:61
  1412.3 5.4 collective-permute-start
  1455.7 28.5 %all-to-all-start.1 = ((bf16[32,2,7168]{2,1,0:T(2,128)(2,1)}), bf16[32,2,7168]{2,1,0:T(2,128)(2,1)S(1)}, u32[]{:S(2)}, u32[]{:S(2)}) async-start(bf16[32,2,7168]{2,1,0:T(2,128)(2,1)} %reshape.139), calls=%async_computation.1 | async-start | bytes 1835008 | tf_op jit(solution)/shard_map/while/body/eval_jaxpr/all_to_all | solution.py:61
  1486.0 5.4 collective-permute-start
  1529.5 28.5 %all-to-all-start.1 = ((bf16[32,2,7168]{2,1,0:T(2,128)(2,1)}), bf16[32,2,7168]{2,1,0:T(2,128)(2,1)S(1)}, u32[]{:S(2)}, u32[]{:S(2)}) async-start(bf16[32,2,7168]{2,1,0:T(2,128)(2,1)} %reshape.139), calls=%async_computation.1 | async-start | bytes 1835008 | tf_op jit(solution)/shard_map/while/body/eval_jaxpr/all_to_all | solution.py:61
  1559.8 5.4 collective-permute-start
  1603.2 28.5 %all-to-all-start.1 = ((bf16[32,2,7168]{2,1,0:T(2,128)(2,1)}), bf16[32,2,7168]{2,1,0:T(2,128)(2,1)S(1)}, u32[]{:S(2)}, u32[]{:S(2)}) async-start(bf16[32,2,7168]{2,1,0:T(2,128)(2,1)} %reshape.139), calls=%async_computation.1 | async-start | bytes 1835008 | tf_op jit(solution)/shard_map/while/body/eval_jaxpr/all_to_all | solution.py:61
  1633.6 5.4 collective-permute-start
  1677.0 28.5 %all-to-all-start.1 = ((bf16[32,2,7168]{2,1,0:T(2,128)(2,1)}), bf16[32,2,7168]{2,1,0:T(2,128)(2,1)S(1)}, u32[]{:S(2)}, u32[]{:S(2)}) async-start(bf16[32,2,7168]{2,1,0:T(2,128)(2,1)} %reshape.139), calls=%async_computation.1 | async-start | bytes 1835008 | tf_op jit(solution)/shard_map/while/body/eval_jaxpr/all_to_all | solution.py:61
  1707.3 5.4 collective-permute-start
where the time goes:
time: 1720 us; the launch traced here: 1710 us
  blocking collectives  680 us (40%)
  waiting for transfers between devices  585 us (34%)
  starting transfers between devices  181 us (11%)
  matrix products  140 us (8%)
  local copies, waits for them, and re-layouts  74.6 us (4%)
  other arithmetic  48.8 us (3%)
    all_to_all x23, blocking collectives, apply_layer(): lax.all_to_all(outgoing, 'expert', split_axis=0, concat_axis=0, tiled=True)  680 us
    all_to_all x23, waiting for transfers between devices, apply_layer(): lax.all_to_all(part, 'expert', split_axis=0, concat_axis=0, tiled=True)  512 us
    all_to_all x23, starting transfers between devices, apply_layer(): lax.all_to_all(part, 'expert', split_axis=0, concat_axis=0, tiled=True)  127 us
    ppermute x23, waiting for transfers between devices, from_behind(): lax.ppermute(value, axis, [(source, source + steps) for source in range(f...  72.7 us
    dot_general x23, matrix products, expert_part(): jnp.dot(hidden, down_rows, preferred_element_type=jnp.float32)  66.1 us
    ppermute x23, starting transfers between devices, from_behind(): lax.ppermute(value, axis, [(source, source + steps) for source in range(f...  54.6 us
    dot_general x23, matrix products, expert_part(): gate = jnp.dot(flat, gate_cols, preferred_element_type=jnp.float32)  45 us
  transfers between devices with their start and end apart: 46, of which 46 were waited for; matrix products, arithmetic and copies ran while one was open for 1% of the time, Pallas kernels for 0%

commit v1 on v0

v1 whole, which is shorter than its diff:
```python
import functools

import jax
import jax.numpy as jnp
from jax import lax
from jax.experimental import pallas as pl
from jax.experimental.pallas import tpu as pltpu
from jax.sharding import PartitionSpec as P

GROUP = 8
MESH = pl.DeviceIdType.MESH
F32 = jnp.float32
BF16 = jnp.bfloat16


def arrived(ref, sem):
    pltpu.make_async_copy(ref, ref, sem).wait()


def kernel(
    n_pipe, width, inp, wg, wu, wd, gains, table, out,
    gate, up, down, xin, ssin, tabs, perm, perm_t, weight,
    dsend, drecv, rsend, rrecv, own, hbuf, ysend, yrecv, xsend, sssend,
    wsend_sem, wrecv_sem, isend_sem, irecv_sem, tsend_sem, trecv_sem,
    dsend_sem, drecv_sem, rsend_sem, rrecv_sem, hsend_sem, hrecv_sem, ysend_sem, yrecv_sem,
    xsend_sem, xrecv_sem, ssend_sem, srecv_sem, osend_sem, orecv_sem, local_sem,
):
    feat = width // GROUP
    pairs = inp.shape[0] // 16
    s = lax.axis_index("pipe")
    e = lax.axis_index("expert")
    k = e // GROUP
    j = e % GROUP
    here = k * GROUP

    def member(steps):
        return here + lax.rem(j + steps + GROUP, GROUP)

    def other(steps):
        return lax.rem(k + steps + 4, 4) * GROUP + j

    def send(src, dst, send_sem, recv_sem, section, place):
        copy = pltpu.make_async_remote_copy(
            src_ref=src, dst_ref=dst, send_sem=send_sem, recv_sem=recv_sem,
            device_id=(section, place), device_id_type=MESH,
        )
        copy.start()

    barrier = pltpu.get_barrier_semaphore()
    for d in range(1, GROUP):
        pl.semaphore_signal(barrier, inc=1, device_id=(s, member(d)), device_id_type=MESH)
    for d in range(1, 4):
        pl.semaphore_signal(barrier, inc=1, device_id=(s, other(d)), device_id_type=MESH)

    @pl.when(s > 0)
    def _():
        for d in range(GROUP):
            pl.semaphore_signal(barrier, inc=1, device_id=(s - 1, member(d)), device_id_type=MESH)

    @pl.when(s < n_pipe - 1)
    def _():
        for d in range(GROUP):
            pl.semaphore_signal(barrier, inc=1, device_id=(s + 1, member(d)), device_id_type=MESH)

    inner = (s > 0) & (s < n_pipe - 1)

    @pl.when(inner)
    def _():
        pl.semaphore_wait(barrier, 3 * GROUP + 2)

    @pl.when(jnp.logical_not(inner))
    def _():
        pl.semaphore_wait(barrier, 2 * GROUP + 2)

    lane = lax.broadcasted_iota(jnp.int32, (8, 128), 1)
    ids = table[0]
    rank = jnp.zeros((8, 128), F32)
    for step in range(1, 8):
        same = (pltpu.roll(ids, step, 1) == ids) & (lane % 8 >= step)
        rank = rank + jnp.where(same, 1.0, 0.0)
    group_index = k.astype(F32)
    relative = ids - group_index + jnp.where(ids < group_index, 4.0, 0.0)
    block = ((lane % 64) // 8).astype(F32)
    mine = lane // 16 == j
    tabs[0, 0] = jnp.where(mine, relative * 16.0 + block * 2.0 + rank, 0.0)
    tabs[0, 1] = jnp.where(mine, table[1], 0.0)
    tabs[0, 2] = jnp.where(mine, table[2], 0.0)
    for d in range(1, GROUP):
        send(tabs.at[0], tabs.at[d], tsend_sem, trecv_sem, s, member(d))

    def cols(d):
        return pl.ds(pl.multiple_of(lax.rem(j + d, GROUP) * feat, 128), feat)

    half = j // 4
    quarter = j % 4

    @pl.when(s == 0)
    def _():
        for d in range(1, GROUP):
            send(
                inp.at[pl.ds(0, 16), cols(d)], xin.at[half, quarter],
                isend_sem.at[0], irecv_sem.at[0], s, member(d),
            )
        pltpu.make_async_copy(inp.at[pl.ds(0, 16), cols(0)], xin.at[half, quarter], irecv_sem.at[0]).start()

    for d in range(1, GROUP):
        rows = cols(d)
        send(wg.at[rows, :], gate.at[d], wsend_sem.at[0], wrecv_sem.at[0], s, member(d))
        send(wu.at[rows, :], up.at[d], wsend_sem.at[1], wrecv_sem.at[1], s, member(d))
    own_gate = pltpu.make_async_copy(wg.at[cols(0), :], gate.at[0], local_sem.at[0])
    own_up = pltpu.make_async_copy(wu.at[cols(0), :], up.at[0], local_sem.at[1])
    own_down = pltpu.make_async_copy(wd.at[:, cols(0)], down.at[0], local_sem.at[2])
    own_gate.start()
    own_up.start()
    own_down.start()
    for d in range(1, GROUP):
        send(wd.at[:, cols(d)], down.at[d], wsend_sem.at[2], wrecv_sem.at[2], s, member(d))

    @pl.when(s == 0)
    def _():
        @pl.loop(1, pairs)
        def _(p):
            rows = pl.ds(pl.multiple_of(p * 16, 16), 16)
            for d in range(1, GROUP):
                send(
                    inp.at[rows, cols(d)], xin.at[2 * p + half, quarter],
                    isend_sem.at[p], irecv_sem.at[p], s, member(d),
                )
            pltpu.make_async_copy(inp.at[rows, cols(0)], xin.at[2 * p + half, quarter], irecv_sem.at[p]).start()

    arrived(tabs.at[pl.ds(1, 7)], trecv_sem)
    total = tabs[0]
    for d in range(1, GROUP):
        total = total + tabs[d]
    sub64 = lax.broadcasted_iota(jnp.int32, (64, 64), 0)
    lane64 = lax.broadcasted_iota(jnp.int32, (64, 64), 1)
    eye = sub64 == lane64
    arrived(tabs.at[pl.ds(1, 7)], tsend_sem)
    tabs[0] = total

    @pl.loop(0, pairs)
    def _(p):
        for h in range(2):
            u = 2 * p + h
            rows = []
            for field in range(3):
                row = tabs[0, field, pl.ds(p, 1), :]
                row = jnp.broadcast_to(row, (8, 128))
                if h:
                    row = pltpu.roll(row, 64, 1)
                rows.append(row)
            place = jnp.broadcast_to(rows[0][0:1, 0:64], (64, 64))
            scale = jnp.broadcast_to(rows[1][0:1, 0:64], (64, 64))
            perm[u] = jnp.where(place == sub64.astype(F32), 1.0, 0.0).astype(BF16)
            place_col = jnp.sum(jnp.where(eye, place, 0.0), axis=1, keepdims=True)
            perm_t[u] = jnp.where(place_col == lane64.astype(F32), 1.0, 0.0).astype(BF16)
            weight[u] = jnp.sum(jnp.where(eye, scale, 0.0), axis=1, keepdims=True)

            @pl.when(s == 0)
            def _():
                ssin[u] = jnp.zeros((GROUP, 8, 128), F32)
                ssin[u, 0] = rows[2]

    def home_out(h, p):
        u = 2 * p + h

        @pl.when(s > 0)
        def _():
            arrived(xin.at[u], xrecv_sem.at[u])
            arrived(ssin.at[u], srecv_sem.at[u])

        squares = ssin[u, 0]
        for d in range(1, GROUP):
            squares = squares + ssin[u, d]
        row = jnp.broadcast_to(squares[0:1, 0:64], (64, 64))
        col = jnp.sum(jnp.where(eye, row, 0.0), axis=1, keepdims=True)
        scale = lax.rsqrt(col * (1.0 / width) + 1e-06)
        normed = (xin[u].reshape(64, feat).astype(F32) * scale * gains[pl.ds(j, 1), :]).astype(BF16)
        ordered = jnp.dot(perm[u], normed, preferred_element_type=F32).astype(BF16)
        dsend[h] = ordered.reshape(4, 16, feat)
        for d in range(1, 4):
            send(dsend.at[h, d], drecv.at[h, d], dsend_sem.at[h], drecv_sem.at[h], s, other(d))
        drecv[h, 0] = dsend[h, 0]

    def first_products(h):
        arrived(drecv.at[h, pl.ds(1, 3)], drecv_sem.at[h])
        tokens = drecv[h].reshape(64, feat)
        for d in (4, 3, 5, 2, 6, 1, 7, 0):
            both = jnp.concatenate([gate[d], up[d]], axis=1)
            part = jnp.dot(tokens, both, preferred_element_type=F32)
            if d:
                rsend[h, d - 1] = part.astype(BF16)
                send(rsend.at[h, d - 1], rrecv.at[h, d - 1], rsend_sem.at[h], rrecv_sem.at[h], s, member(-d))
            else:
                own[h] = part

    def hidden_units(h):
        arrived(rrecv.at[h], rrecv_sem.at[h])
        both = own[h]
        for d in range(7):
            both = both + rrecv[h, d].astype(F32)
        value = both[:, 0:128]
        hidden = (value / (1.0 + jnp.exp(-value)) * both[:, 128:256]).astype(BF16)
        hbuf[h, 0] = hidden
        for d in (4, 3, 5, 2, 6, 1, 7):
            send(hbuf.at[h, 0], hbuf.at[h, d], hsend_sem.at[h], hrecv_sem.at[h], s, member(d))

    def second_product(h):
        arrived(hbuf.at[h, pl.ds(1, 7)], hrecv_sem.at[h])
        hidden = jnp.concatenate([hbuf[h, d] for d in range(GROUP)], axis=1)
        part = jnp.dot(hidden, down[...].reshape(GROUP * 128, feat), preferred_element_type=F32)
        ysend[h] = part.astype(BF16).reshape(4, 16, feat)
        for d in range(1, 4):
            send(ysend.at[h, d], yrecv.at[h, d], ysend_sem.at[h], yrecv_sem.at[h], s, other(-d))
        yrecv[h, 0] = ysend[h, 0]

    def home_in(h, p):
        u = 2 * p + h
        arrived(yrecv.at[h, pl.ds(1, 3)], yrecv_sem.at[h])
        gathered = jnp.dot(perm_t[u], yrecv[h].reshape(64, feat), preferred_element_type=F32)
        fresh = (xin[u].reshape(64, feat).astype(F32) + weight[u] * gathered).astype(BF16)
        xsend[h] = fresh.reshape(4, 16, feat)

        @pl.when(s < n_pipe - 1)
        def _():
            send(xsend.at[h], xin.at[u], xsend_sem.at[h], xrecv_sem.at[u], s + 1, e)
            wide = fresh.astype(F32)
            squares = wide * wide
            acc = squares[:, 0:128]
            for c in range(1, feat // 128):
                acc = acc + squares[:, c * 128:(c + 1) * 128]
            col = jnp.sum(acc, axis=1, keepdims=True)
            row = jnp.sum(jnp.where(eye, jnp.broadcast_to(col, (64, 64)), 0.0), axis=0, keepdims=True)
            row = jnp.concatenate([row, row], axis=1)
            sssend[h] = jnp.broadcast_to(row, (8, 128))
            for d in range(GROUP):
                send(sssend.at[h], ssin.at[u, d], ssend_sem.at[h], srecv_sem.at[u], s + 1, member(d))

        rows = pl.ds(pl.multiple_of(p * 16, 16), 16)
        for q in range(4):
            m = 4 * h + q

            @pl.when(m == j)
            def _():
                pltpu.make_async_copy(xsend.at[h, q], out.at[rows, cols(0)], osend_sem.at[h]).start()

            @pl.when(m != j)
            def _():
                send(xsend.at[h, q], out.at[rows, cols(0)], osend_sem.at[h], orecv_sem.at[p], s, here + m)

    own_gate.wait()
    own_up.wait()
    arrived(gate.at[pl.ds(1, 7)], wrecv_sem.at[0])
    arrived(up.at[pl.ds(1, 7)], wrecv_sem.at[1])
    own_down.wait()
    arrived(down.at[pl.ds(1, 7)], wrecv_sem.at[2])

    @pl.loop(0, pairs)
    def _(p):
        @pl.when(s == 0)
        def _():
            arrived(xin.at[pl.ds(2 * p, 2)], irecv_sem.at[p])

        for h in range(2):
            home_out(h, p)
        for h in range(2):
            first_products(h)
        for h in range(2):
            hidden_units(h)
        for h in range(2):
            second_product(h)
        for h in range(2):
            home_in(h, p)
        for h in range(2):
            arrived(dsend.at[h, pl.ds(1, 3)], dsend_sem.at[h])
            arrived(rsend.at[h], rsend_sem.at[h])
            arrived(hbuf.at[h, pl.ds(1, 7)], hsend_sem.at[h])
            arrived(ysend.at[h, pl.ds(1, 3)], ysend_sem.at[h])
            arrived(xsend.at[h], osend_sem.at[h])

            @pl.when(s < n_pipe - 1)
            def _():
                arrived(xsend.at[h], xsend_sem.at[h])
                arrived(ssin.at[0], ssend_sem.at[h])

    @pl.loop(0, pairs)
    def _(p):
        arrived(out.at[pl.ds(pl.multiple_of(p * 16, 16), 16), pl.ds(0, 7 * feat)], orecv_sem.at[p])

        @pl.when(s == 0)
        def _():
            arrived(inp.at[pl.ds(pl.multiple_of(p * 16, 16), 16), pl.ds(0, 7 * feat)], isend_sem.at[p])

    arrived(gate.at[pl.ds(1, 7)], wsend_sem.at[0])
    arrived(up.at[pl.ds(1, 7)], wsend_sem.at[1])
    arrived(down.at[pl.ds(1, 7)], wsend_sem.at[2])


def local(inputs, norm_gains, w_gate, w_up, w_down, expert_ids, gate_weights):
    micro, rows, width = inputs.shape
    feat = width // GROUP
    pairs = micro // 2
    units = 2 * pairs
    n_pipe = lax.axis_size("pipe")
    squares = jnp.sum(jnp.square(inputs.astype(F32)), axis=-1)
    fields = jnp.stack([expert_ids[0, :, :, 0].astype(F32), gate_weights[0], squares])
    table = jnp.tile(fields.reshape(3, pairs, 16), (1, 1, 8))
    table = jnp.pad(table, ((0, 0), (0, 8 - pairs), (0, 0)))
    anywhere = pl.BlockSpec(memory_space=pl.ANY)
    vmem = pl.BlockSpec(memory_space=pltpu.VMEM)
    dma = pltpu.SemaphoreType.DMA
    states = pl.pallas_call(
        functools.partial(kernel, n_pipe, width),
        out_shape=jax.ShapeDtypeStruct((micro * rows, width), BF16),
        in_specs=[anywhere] * 4 + [vmem] * 2,
        out_specs=anywhere,
        scratch_shapes=[
            pltpu.VMEM((GROUP, feat, 128), BF16),
            pltpu.VMEM((GROUP, feat, 128), BF16),
            pltpu.VMEM((GROUP, 128, feat), BF16),
            pltpu.VMEM((units, 4, 16, feat), BF16),
            pltpu.VMEM((units, GROUP, 8, 128), F32),
            pltpu.VMEM((GROUP, 3, 8, 128), F32),
            pltpu.VMEM((units, 64, 64), BF16),
            pltpu.VMEM((units, 64, 64), BF16),
            pltpu.VMEM((units, 64, 1), F32),
            pltpu.VMEM((2, 4, 16, feat), BF16),
            pltpu.VMEM((2, 4, 16, feat), BF16),
            pltpu.VMEM((2, 7, 64, 256), BF16),
            pltpu.VMEM((2, 7, 64, 256), BF16),
            pltpu.VMEM((2, 64, 256), F32),
            pltpu.VMEM((2, GROUP, 64, 128), BF16),
            pltpu.VMEM((2, 4, 16, feat), BF16),
            pltpu.VMEM((2, 4, 16, feat), BF16),
            pltpu.VMEM((2, 4, 16, feat), BF16),
            pltpu.VMEM((2, 8, 128), F32),
            dma((3,)), dma((3,)), dma((pairs,)), dma((pairs,)), dma, dma,
            dma((2,)), dma((2,)), dma((2,)), dma((2,)), dma((2,)), dma((2,)), dma((2,)), dma((2,)),
            dma((2,)), dma((units,)), dma((2,)), dma((units,)), dma((2,)), dma((pairs,)), dma((3,)),
        ],
        compiler_params=pltpu.CompilerParams(
            collective_id=0, has_side_effects=True, vmem_limit_bytes=56 * 1024 * 1024
        ),
    )(
        inputs.reshape(micro * rows, width), w_gate[0], w_up[0], w_down[0],
        norm_gains.reshape(GROUP, feat), table,
    )
    return states.reshape(1, micro, rows, width)


def solution(mesh):
    return jax.shard_map(
        local,
        mesh=mesh,
        in_specs=(
            P(None, "expert", None),
            P("pipe", None),
            P("pipe", None, "expert"),
            P("pipe", None, "expert"),
            P("pipe", "expert", None),
            P("pipe", None, "expert", None),
            P("pipe", None, "expert"),
        ),
        out_specs=P("pipe", None, "expert", None),
        check_vma=False,
    )
```

time: 1720 us -> 533 us (0.31)
  the two profiles are of different devices: /device:TPU:1 before, /device:TPU:39 now
where the time goes in v1:
time: 533 us
  Pallas kernels  523 us (98%)
  local copies, waits for them, and re-layouts  5.72 us (1%)
    pallas_call x1, Pallas kernels, local(): pl.pallas_call(functools.partial(kernel, n_pipe, width), out_shape=jax.Sh...  523 us

profile of v1, /device:TPU:39, one launch (start us, length us, event | category | flops | bytes accessed | tf_op | source)
XLA Modules:
  0.0 532.6 jit_solution(6080949444788084659)
XLA Ops:
  0.0 0.0 copy-start
  0.0 0.7 convert_element_type.17
  0.7 0.1 copy.10
  0.8 0.1 convert_element_type.18
  0.8 0.8 copy.11
  1.6 0.1 stack.9
  1.7 2.0 multiply_reduce_fusion
  3.6 0.1 stack.10
  3.7 0.5 broadcast.5
  4.2 0.0 copy-done
  4.2 0.7 reduce.3
  4.9 0.6 reshape.29.gains
  5.6 0.7 tile.12.table
  6.3 523.5 %shard_map.73 = bf16[128,7168]{1,0:T(8,128)(2,1)} custom-call(bf16[128,7168]{1,0:T(8,128)(2,1)} %bitcast.13, bf16[7168,128]{1,0:T(8,128)(2,1)} %bitcast.15, bf16[7168,128]{1,0:T(8,128)(2,1)} %bitcast.16, bf16[128,7168]{1,0:T(8,128)(2,1)} %bitcast.17, f32[8,896]{1,0:T(8,128)} %reshape.29.gains, f32[3,8,128]{2,1,0:T(8,128)} %tile.12.table), custom_call_target="tpu_custom_call" | custom-call | tf_op jit(solution)/shard_map/pallas_call | solution.py:312
  529.7 2.8 copy.13
  (2 shorter events, 0.0 us)
Async XLA Ops:
  0.0 4.2 copy-start

commit v2 on v0

v2 whole, which is shorter than its diff:
```python
import functools

import jax
import jax.numpy as jnp
from jax import lax
from jax.experimental import pallas as pl
from jax.experimental.pallas import tpu as pltpu
from jax.sharding import PartitionSpec as P

GROUP = 8
MESH = pl.DeviceIdType.MESH
F32 = jnp.float32
BF16 = jnp.bfloat16


def arrived(ref, sem):
    pltpu.make_async_copy(ref, ref, sem).wait()


def kernel(
    n_pipe, width, inp, wg, wu, wd, gains, table, out,
    gate, up, down, xin, xcur, tabs, alltab, allgain, perm, perm_t, weight, obuf,
    sssend, ssin, dsend, drecv, rsend, rrecv, own, psend, precv, hbuf, ysend, yrecv, xsend,
    wsend_sem, wrecv_sem, fsend_sem, frecv_sem, msend_sem, mrecv_sem, isend_sem, irecv_sem,
    tsend_sem, trecv_sem, asend_sem, arecv_sem, gsend_sem, grecv_sem,
    ssend_sem, srecv_sem, dsend_sem, drecv_sem, rsend_sem, rrecv_sem, psend_sem, precv_sem,
    hsend_sem, hrecv_sem, ysend_sem, yrecv_sem, xsend_sem, xrecv_sem, osend_sem, orecv_sem,
    local_sem, go_sem,
):
    feat = width // GROUP
    chips = n_pipe // 2
    s = lax.axis_index("pipe")
    e = lax.axis_index("expert")
    k = e // GROUP
    j = e % GROUP
    here = k * GROUP
    y = j % 4
    parity = j // 4
    chip = s // 2
    core = s % 2
    mate = chip * 2 + 1 - core
    ahead = lax.rem(chip + 1, chips) * 2 + core
    behind = lax.rem(chip + chips - 1, chips) * 2 + core

    def number(steps):
        return lax.rem(parity + steps // 4, 2) * 4 + lax.rem(y + steps, 4)

    def member(steps):
        return here + number(steps)

    def row_member(steps):
        return here + parity * 4 + lax.rem(y + steps + 4, 4)

    def other(steps):
        return lax.rem(k + steps + 4, 4) * GROUP + j

    def cols(d):
        return pl.ds(pl.multiple_of(number(d) * feat, 128), feat)

    def send(src, dst, send_sem, recv_sem, section, place):
        copy = pltpu.make_async_remote_copy(
            src_ref=src, dst_ref=dst, send_sem=send_sem, recv_sem=recv_sem,
            device_id=(section, place), device_id_type=MESH,
        )
        copy.start()

    barrier = pltpu.get_barrier_semaphore()
    for d in range(1, GROUP):
        pl.semaphore_signal(barrier, inc=1, device_id=(s, member(d)), device_id_type=MESH)
    for d in range(1, 4):
        pl.semaphore_signal(barrier, inc=1, device_id=(s, other(d)), device_id_type=MESH)
    for d in range(1, n_pipe):
        pl.semaphore_signal(barrier, inc=1, device_id=(lax.rem(s + d, n_pipe), e), device_id_type=MESH)
    pl.semaphore_wait(barrier, GROUP - 1 + 3 + n_pipe - 1)

    def send_first_weights():
        for d in range(1, GROUP):
            send(wg.at[cols(d), :], gate.at[s, d], wsend_sem.at[0], wrecv_sem.at[0], s, member(d))
            send(wu.at[cols(d), :], up.at[s, d], wsend_sem.at[1], wrecv_sem.at[1], s, member(d))

    def send_last_weights():
        for d in range(1, GROUP):
            send(wd.at[:, cols(d)], down.at[s, d], wsend_sem.at[2], wrecv_sem.at[2], s, member(d))

    pl.when(core == 0)(send_first_weights)
    own_gate = pltpu.make_async_copy(wg.at[cols(0), :], gate.at[s, 0], local_sem.at[0])
    own_up = pltpu.make_async_copy(wu.at[cols(0), :], up.at[s, 0], local_sem.at[1])
    own_down = pltpu.make_async_copy(wd.at[:, cols(0)], down.at[s, 0], local_sem.at[2])
    own_gate.start()
    own_up.start()
    own_down.start()

    my_rows = pl.ds(pl.multiple_of(s * 16, 16), 16)
    half = j // 4
    quarter = j % 4
    for d in range(1, GROUP):
        send(inp.at[my_rows, cols(d)], xin.at[half, quarter], isend_sem, irecv_sem, s, member(d))
    pltpu.make_async_copy(inp.at[my_rows, cols(0)], xin.at[half, quarter], irecv_sem).start()

    lane = lax.broadcasted_iota(jnp.int32, (8, 128), 1)
    ids = table[0]
    rank = jnp.zeros((8, 128), F32)
    for step in range(1, 8):
        same = (pltpu.roll(ids, step, 1) == ids) & (lane % 8 >= step)
        rank = rank + jnp.where(same, 1.0, 0.0)
    group_index = k.astype(F32)
    relative = ids - group_index + jnp.where(ids < group_index, 4.0, 0.0)
    block = ((lane % 64) // 8).astype(F32)
    mine = lane // 16 == j
    tabs[0, 0] = jnp.where(mine, relative * 16.0 + block * 2.0 + rank, 0.0)
    tabs[0, 1] = jnp.where(mine, table[1], 0.0)
    for d in range(1, GROUP):
        send(tabs.at[0], tabs.at[d], tsend_sem, trecv_sem, s, member(d))
    allgain[s] = gains[...]
    for d in range(1, n_pipe):
        send(allgain.at[s], allgain.at[s], gsend_sem, grecv_sem, lax.rem(s + d, n_pipe), e)
    arrived(tabs.at[pl.ds(1, 7)], trecv_sem)
    total = tabs[0]
    for d in range(1, GROUP):
        total = total + tabs[d]
    alltab[s] = total
    for d in range(1, n_pipe):
        send(alltab.at[s], alltab.at[s], asend_sem, arecv_sem, lax.rem(s + d, n_pipe), e)

    sub64 = lax.broadcasted_iota(jnp.int32, (64, 64), 0)
    lane64 = lax.broadcasted_iota(jnp.int32, (64, 64), 1)
    eye = sub64 == lane64
    arrived(alltab.at[pl.ds(0, n_pipe - 1)], arecv_sem)
    arrived(allgain.at[pl.ds(0, n_pipe - 1)], grecv_sem)

    @pl.loop(0, n_pipe)
    def _(m):
        for h in range(2):
            rows = []
            for field in range(2):
                row = jnp.broadcast_to(alltab[m, field, pl.ds(s, 1), :], (8, 128))
                if h:
                    row = pltpu.roll(row, 64, 1)
                rows.append(jnp.broadcast_to(row[0:1, 0:64], (64, 64)))
            place, scale = rows
            perm[m, h] = jnp.where(place == sub64.astype(F32), 1.0, 0.0).astype(BF16)
            place_col = jnp.sum(jnp.where(eye, place, 0.0), axis=1, keepdims=True)
            perm_t[m, h] = jnp.where(place_col == lane64.astype(F32), 1.0, 0.0).astype(BF16)
            weight[m, h] = jnp.sum(jnp.where(eye, scale, 0.0), axis=1, keepdims=True)

    def slot(m, h):
        return lax.rem(m, 2) * 2 + h

    def send_squares(h, m, wide):
        b = slot(m, h)
        squares = wide * wide
        acc = squares[:, 0:128]
        for c in range(1, feat // 128):
            acc = acc + squares[:, c * 128:(c + 1) * 128]
        col = jnp.sum(acc, axis=1, keepdims=True)
        row = jnp.sum(jnp.where(eye, jnp.broadcast_to(col, (64, 64)), 0.0), axis=0, keepdims=True)
        row = jnp.broadcast_to(jnp.concatenate([row, row], axis=1), (8, 128))
        sssend[b] = row
        ssin[b, 0] = row
        for d in (6, 2, 5, 7, 1, 3, 4):
            send(sssend.at[b], ssin.at[b, d], ssend_sem.at[b], srecv_sem.at[b], s, member(d))

    arrived(xin, irecv_sem)
    for h in range(2):
        wide = xin[h].reshape(64, feat).astype(F32)
        xcur[h] = wide
        send_squares(h, 0, wide)

    def pass_on(tick):
        @pl.loop(0, chips)
        def _(i):
            m = 2 * i + core
            for way in range(2):
                if way == 0:
                    hops = lax.rem(chip - i + chips, chips)
                    target = ahead
                else:
                    hops = lax.rem(i - chip + chips, chips)
                    target = behind
                cc = tick - 6 * i - hops

                if way == 0:
                    @pl.when((m == s) & (cc == 0))
                    def _():
                        own_gate.wait()
                        own_up.wait()

                        @pl.when(core == 1)
                        def _():
                            arrived(gate.at[s, pl.ds(1, 7)], wrecv_sem.at[0])
                            arrived(up.at[s, pl.ds(1, 7)], wrecv_sem.at[1])

                    @pl.when((m == s) & (cc == 4))
                    def _():
                        own_down.wait()
                        arrived(down.at[s, pl.ds(1, 7)], wrecv_sem.at[2])

                def move(ref, kind):
                    sem = frecv_sem.at[m, 2 * cc + way]

                    @pl.when(hops > 0)
                    def _():
                        arrived(ref, sem)

                    @pl.when(hops < chips - 1)
                    def _():
                        send(ref, ref, fsend_sem.at[i, way, kind // 2], sem, target, e)

                    send(ref, ref, msend_sem.at[i, kind], mrecv_sem.at[m, kind], mate, e)

                @pl.when((cc >= 0) & (cc < 4))
                def _():
                    move((gate, up)[way].at[m, pl.ds(2 * cc, 2)], way)

                @pl.when((cc >= 4) & (cc < 6))
                def _():
                    move(down.at[m, pl.ds(2 * cc - 8 + 4 * way, 2)], 2)

    @pl.when(core == 0)
    def _():
        arrived(gate.at[s, pl.ds(1, 7)], wrecv_sem.at[0])
        arrived(up.at[s, pl.ds(1, 7)], wrecv_sem.at[1])
        send_last_weights()
        pl.semaphore_signal(go_sem, inc=1, device_id=(mate, e), device_id_type=MESH)

        @pl.loop(0, 9)
        def _(tick):
            pass_on(tick)

    @pl.when(core == 1)
    def _():
        pl.semaphore_wait(go_sem, 1)
        send_first_weights()
        send_last_weights()

    def pass_on_beside(m, step):
        @pl.when((core == 0) | (m > 0))
        def _():
            pass_on(9 + 3 * (m - core) + step)

        @pl.when((core == 1) & (m == 0))
        def _():
            @pl.loop(3 * step, 3 * step + 3)
            def _(tick):
                pass_on(tick)

    def home_out(h, m):
        b = slot(m, h)
        arrived(ssin.at[b, pl.ds(1, 7)], srecv_sem.at[b])
        squares = ssin[b, 0]
        for d in range(1, GROUP):
            squares = squares + ssin[b, d]
        row = jnp.broadcast_to(squares[0:1, 0:64], (64, 64))
        col = jnp.sum(jnp.where(eye, row, 0.0), axis=1, keepdims=True)
        scale = lax.rsqrt(col * (1.0 / width) + 1e-06)
        normed = (xcur[h] * scale * allgain[m, pl.ds(j, 1), :]).astype(BF16)
        ordered = jnp.dot(perm[m, h], normed, preferred_element_type=F32).astype(BF16)
        dsend[b] = ordered.reshape(4, 16, feat)
        for d in (2, 1, 3):
            send(dsend.at[b, d], drecv.at[b, d], dsend_sem.at[b], drecv_sem.at[b], s, other(d))
        drecv[b, 0] = dsend[b, 0]

    def first_products(h, m):
        b = slot(m, h)
        arrived(drecv.at[b, pl.ds(1, 3)], drecv_sem.at[b])
        tokens = drecv[b].reshape(64, feat)
        for d in (2, 1, 3, 0):
            for half_at in range(2):
                both = jnp.concatenate([gate[m, 4 * half_at + d], up[m, 4 * half_at + d]], axis=1)
                part = jnp.dot(tokens, both, preferred_element_type=F32)
                if d:
                    rsend[b, d - 1, half_at] = part.astype(BF16)
                else:
                    own[b, half_at] = part
            if d:
                send(rsend.at[b, d - 1], rrecv.at[b, d - 1], rsend_sem.at[b], rrecv_sem.at[b], s, row_member(-d))

    def row_sums(h, m):
        b = slot(m, h)
        arrived(rrecv.at[b], rrecv_sem.at[b])
        for half_at in range(2):
            both = own[b, half_at]
            for d in range(3):
                both = both + rrecv[b, d, half_at].astype(F32)
            own[b, half_at] = both
            psend[b, 1 - half_at] = both.astype(BF16)
        send(psend.at[b], precv.at[b], psend_sem.at[b], precv_sem.at[b], s, member(4))

    def hidden_units(h, m):
        b = slot(m, h)
        arrived(precv.at[b], precv_sem.at[b])
        for half_at in range(2):
            both = own[b, half_at] + precv[b, half_at].astype(F32)
            value = both[:, 0:128]
            hbuf[b, 0, half_at] = (value / (1.0 + jnp.exp(-value)) * both[:, 128:256]).astype(BF16)
        for d in (2, 1, 3):
            send(hbuf.at[b, 0], hbuf.at[b, d], hsend_sem.at[b], hrecv_sem.at[b], s, row_member(d))

    def second_product(h, m):
        b = slot(m, h)
        arrived(hbuf.at[b, pl.ds(1, 3)], hrecv_sem.at[b])
        hidden = jnp.concatenate([hbuf[b, d, half_at] for half_at in range(2) for d in range(4)], axis=1)
        part = jnp.dot(hidden, down[m].reshape(GROUP * 128, feat), preferred_element_type=F32)
        ysend[b] = part.astype(BF16).reshape(4, 16, feat)
        for d in (2, 1, 3):
            send(ysend.at[b, d], yrecv.at[b, d], ysend_sem.at[b], yrecv_sem.at[b], s, other(-d))
        yrecv[b, 0] = ysend[b, 0]

    def home_in(h, m):
        b = slot(m, h)
        arrived(yrecv.at[b, pl.ds(1, 3)], yrecv_sem.at[b])
        gathered = jnp.dot(perm_t[m, h], yrecv[b].reshape(64, feat), preferred_element_type=F32)
        fresh = (xcur[h] + weight[m, h] * gathered).astype(BF16)
        wide = fresh.astype(F32)
        xcur[h] = wide

        @pl.when(m < n_pipe - 1)
        def _():
            send_squares(h, m + 1, wide)

        xsend[b] = fresh.reshape(4, 16, feat)
        for q in range(4):
            owner = 4 * h + q

            @pl.when(owner == j)
            def _():
                pltpu.make_async_copy(xsend.at[b, q], obuf.at[m, :, cols(0)], xsend_sem.at[b]).start()

            @pl.when(owner != j)
            def _():
                send(xsend.at[b, q], obuf.at[m, :, cols(0)], xsend_sem.at[b], xrecv_sem.at[m], s, here + owner)

    def hand_over(m):
        for h in range(2):
            b = slot(m, h)
            arrived(dsend.at[b, pl.ds(1, 3)], dsend_sem.at[b])
            arrived(rsend.at[b], rsend_sem.at[b])
            arrived(psend.at[b], psend_sem.at[b])
            arrived(hbuf.at[b, pl.ds(1, 3)], hsend_sem.at[b])
            arrived(ysend.at[b, pl.ds(1, 3)], ysend_sem.at[b])
            arrived(ssin.at[b, pl.ds(1, 7)], ssend_sem.at[b])
            arrived(xsend.at[b], xsend_sem.at[b])
        arrived(obuf.at[m, :, pl.ds(0, 7 * feat)], xrecv_sem.at[m])

        @pl.when(m == s)
        def _():
            pltpu.make_async_copy(obuf.at[m], out.at[my_rows, :], local_sem.at[3]).start()

        @pl.when(m != s)
        def _():
            send(obuf.at[m], out.at[my_rows, :], osend_sem.at[m], orecv_sem.at[s], m, e)

    @pl.loop(0, n_pipe)
    def _(m):
        for h in range(2):
            home_out(h, m)

        pass_on_beside(m, 0)

        @pl.when(lax.rem(m, 2) != core)
        def _():
            arrived(gate.at[m], mrecv_sem.at[m, 0])
            arrived(up.at[m], mrecv_sem.at[m, 1])

        for h in range(2):
            first_products(h, m)

        @pl.when(m > 0)
        def _():
            hand_over(m - 1)

        for h in range(2):
            row_sums(h, m)

        pass_on_beside(m, 1)

        for h in range(2):
            hidden_units(h, m)

        @pl.when(lax.rem(m, 2) != core)
        def _():
            arrived(down.at[m], mrecv_sem.at[m, 2])

        for h in range(2):
            second_product(h, m)

        pass_on_beside(m, 2)

        for h in range(2):
            home_in(h, m)

    hand_over(n_pipe - 1)

    arrived(tabs.at[pl.ds(1, 7)], tsend_sem)
    arrived(alltab.at[pl.ds(0, n_pipe - 1)], asend_sem)
    arrived(allgain.at[pl.ds(0, n_pipe - 1)], gsend_sem)
    arrived(inp.at[pl.ds(0, 16), pl.ds(0, 7 * feat)], isend_sem)
    arrived(gate.at[s, pl.ds(1, 7)], wsend_sem.at[0])
    arrived(up.at[s, pl.ds(1, 7)], wsend_sem.at[1])
    arrived(down.at[s, pl.ds(1, 7)], wsend_sem.at[2])

    @pl.loop(0, chips)
    def _(i):
        @pl.when(lax.rem(chip - i + chips, chips) < chips - 1)
        def _():
            arrived(gate.at[0], fsend_sem.at[i, 0, 0])
            arrived(down.at[0, pl.ds(0, 4)], fsend_sem.at[i, 0, 1])

        @pl.when(lax.rem(i - chip + chips, chips) < chips - 1)
        def _():
            arrived(up.at[0], fsend_sem.at[i, 1, 0])
            arrived(down.at[0, pl.ds(0, 4)], fsend_sem.at[i, 1, 1])

        arrived(gate.at[0], msend_sem.at[i, 0])
        arrived(up.at[0], msend_sem.at[i, 1])
        arrived(down.at[0], msend_sem.at[i, 2])

    @pl.loop(0, n_pipe)
    def _(m):
        rows = pl.ds(pl.multiple_of(m * 16, 16), 16)

        @pl.when(m == s)
        def _():
            pltpu.make_async_copy(obuf.at[m], out.at[rows, :], local_sem.at[3]).wait()

        @pl.when(m != s)
        def _():
            arrived(obuf.at[m], osend_sem.at[m])
            arrived(out.at[rows, :], orecv_sem.at[m])


def local(inputs, norm_gains, w_gate, w_up, w_down, expert_ids, gate_weights):
    micro, rows, width = inputs.shape
    feat = width // GROUP
    pairs = micro // 2
    n_pipe = lax.axis_size("pipe")
    fields = jnp.stack([expert_ids[0, :, :, 0].astype(F32), gate_weights[0]])
    table = jnp.tile(fields.reshape(2, pairs, 16), (1, 1, 8))
    table = jnp.pad(table, ((0, 0), (0, 8 - pairs), (0, 0)))
    anywhere = pl.BlockSpec(memory_space=pl.ANY)
    vmem = pl.BlockSpec(memory_space=pltpu.VMEM)
    dma = pltpu.SemaphoreType.DMA
    states = pl.pallas_call(
        functools.partial(kernel, n_pipe, width),
        out_shape=jax.ShapeDtypeStruct((micro * rows, width), BF16),
        in_specs=[anywhere] * 4 + [vmem] * 2,
        out_specs=anywhere,
        scratch_shapes=[
            pltpu.VMEM((n_pipe, GROUP, feat, 128), BF16),
            pltpu.VMEM((n_pipe, GROUP, feat, 128), BF16),
            pltpu.VMEM((n_pipe, GROUP, 128, feat), BF16),
            pltpu.VMEM((2, 4, 16, feat), BF16),
            pltpu.VMEM((2, 64, feat), F32),
            pltpu.VMEM((GROUP, 2, 8, 128), F32),
            pltpu.VMEM((n_pipe, 2, 8, 128), F32),
            pltpu.VMEM((n_pipe, GROUP, feat), F32),
            pltpu.VMEM((n_pipe, 2, 64, 64), BF16),
            pltpu.VMEM((n_pipe, 2, 64, 64), BF16),
            pltpu.VMEM((n_pipe, 2, 64, 1), F32),
            pltpu.VMEM((n_pipe, 16, width), BF16),
            pltpu.VMEM((4, 8, 128), F32),
            pltpu.VMEM((4, GROUP, 8, 128), F32),
            pltpu.VMEM((4, 4, 16, feat), BF16),
            pltpu.VMEM((4, 4, 16, feat), BF16),
            pltpu.VMEM((4, 3, 2, 64, 256), BF16),
            pltpu.VMEM((4, 3, 2, 64, 256), BF16),
            pltpu.VMEM((4, 2, 64, 256), F32),
            pltpu.VMEM((4, 2, 64, 256), BF16),
            pltpu.VMEM((4, 2, 64, 256), BF16),
            pltpu.VMEM((4, 4, 2, 64, 128), BF16),
            pltpu.VMEM((4, 4, 16, feat), BF16),
            pltpu.VMEM((4, 4, 16, feat), BF16),
            pltpu.VMEM((4, 4, 16, feat), BF16),
            dma((3,)), dma((3,)), dma((n_pipe // 2, 2, 2)), dma((n_pipe, 12)),
            dma((n_pipe // 2, 3)), dma((n_pipe, 3)), dma, dma,
            dma, dma, dma, dma, dma, dma,
            dma((4,)), dma((4,)), dma((4,)), dma((4,)), dma((4,)), dma((4,)), dma((4,)), dma((4,)),
            dma((4,)), dma((4,)), dma((4,)), dma((4,)), dma((4,)), dma((n_pipe,)), dma((n_pipe,)), dma((n_pipe,)),
            dma((4,)), pltpu.SemaphoreType.REGULAR,
        ],
        compiler_params=pltpu.CompilerParams(
            collective_id=0, has_side_effects=True, vmem_limit_bytes=60 * 1024 * 1024
        ),
    )(
        inputs.reshape(micro * rows, width), w_gate[0], w_up[0], w_down[0],
        norm_gains.reshape(GROUP, feat), table,
    )
    return states.reshape(1, micro, rows, width)


def solution(mesh):
    return jax.shard_map(
        local,
        mesh=mesh,
        in_specs=(
            P(None, "expert", None),
            P("pipe", None),
            P("pipe", None, "expert"),
            P("pipe", None, "expert"),
            P("pipe", "expert", None),
            P("pipe", None, "expert", None),
            P("pipe", None, "expert"),
        ),
        out_specs=P("pipe", None, "expert", None),
        check_vma=False,
    )
```

time: 1720 us -> 427 us (0.25)
  the two profiles are of different devices: /device:TPU:1 before, /device:TPU:39 now
where the time goes in v2:
time: 427 us
  Pallas kernels  419 us (98%)
  local copies, waits for them, and re-layouts  5.63 us (1%)
    pallas_call x1, Pallas kernels, local(): pl.pallas_call(functools.partial(kernel, n_pipe, width), out_shape=jax.Sh...  419 us

profile of v2, /device:TPU:39, one launch (start us, length us, event | category | flops | bytes accessed | tf_op | source)
XLA Modules:
  0.0 426.8 jit_solution(4835737382341131566)
XLA Ops:
  0.0 0.7 convert_element_type.14
  0.7 0.1 copy.10
  0.8 0.1 convert_element_type.15
  0.8 0.8 copy.11
  1.6 0.1 stack.6
  1.7 0.5 broadcast.5
  2.2 1.5 reduce.3
  3.6 0.6 reshape.27.gains
  4.3 0.7 tile.12.table
  4.9 419.0 %shard_map.73 = bf16[128,7168]{1,0:T(8,128)(2,1)} custom-call(bf16[128,7168]{1,0:T(8,128)(2,1)} %bitcast.14, bf16[7168,128]{1,0:T(8,128)(2,1)} %bitcast.15, bf16[7168,128]{1,0:T(8,128)(2,1)} %bitcast.16, bf16[128,7168]{1,0:T(8,128)(2,1)} %bitcast.17, f32[8,896]{1,0:T(8,128)} %reshape.27.gains, f32[2,8,128]{2,1,0:T(8,128)} %tile.12.table), custom_call_target="tpu_custom_call" | custom-call | tf_op jit(solution)/shard_map/pallas_call | solution.py:443
  423.9 2.8 copy.13
  (2 shorter events, 0.0 us)

commit v3 on v2

--- a/solution.py
+++ b/solution.py
@@ -8,6 +8,10 @@
 from jax.sharding import PartitionSpec as P
 
 GROUP = 8
+PIECES = 6
+SKEW = 2
+STRIDE = 4
+FIRST = PIECES + 3 * SKEW
 MESH = pl.DeviceIdType.MESH
 F32 = jnp.float32
 BF16 = jnp.bfloat16
@@ -20,10 +24,10 @@
 def kernel(
     n_pipe, width, inp, wg, wu, wd, gains, table, out,
     gate, up, down, xin, xcur, tabs, alltab, allgain, perm, perm_t, weight, obuf,
-    sssend, ssin, dsend, drecv, rsend, rrecv, own, psend, precv, hbuf, ysend, yrecv, xsend,
+    sssend, ssin, scsend, screcv, dsend, drecv, rsend, rrecv, own, psend, precv, hbuf, ysend, yrecv, xsend,
     wsend_sem, wrecv_sem, fsend_sem, frecv_sem, msend_sem, mrecv_sem, isend_sem, irecv_sem,
     tsend_sem, trecv_sem, asend_sem, arecv_sem, gsend_sem, grecv_sem,
-    ssend_sem, srecv_sem, dsend_sem, drecv_sem, rsend_sem, rrecv_sem, psend_sem, precv_sem,
+    ssend_sem, srecv_sem, dsend_sem, drecv_sem, rsend_sem, rrecv_sem, scsend_sem, screcv_sem, psend_sem, precv_sem,
     hsend_sem, hrecv_sem, ysend_sem, yrecv_sem, xsend_sem, xrecv_sem, osend_sem, orecv_sem,
     local_sem, go_sem,
 ):
@@ -75,14 +79,15 @@
 
     def send_first_weights():
         for d in range(1, GROUP):
-            send(wg.at[cols(d), :], gate.at[s, d], wsend_sem.at[0], wrecv_sem.at[0], s, member(d))
-            send(wu.at[cols(d), :], up.at[s, d], wsend_sem.at[1], wrecv_sem.at[1], s, member(d))
+            send(wg.at[cols(d), :], gate.at[s, d], wsend_sem.at[0], wrecv_sem.at[0, d], s, member(d))
+            send(wu.at[cols(d), :], up.at[s, d], wsend_sem.at[1], wrecv_sem.at[1, d], s, member(d))
 
     def send_last_weights():
         for d in range(1, GROUP):
-            send(wd.at[:, cols(d)], down.at[s, d], wsend_sem.at[2], wrecv_sem.at[2], s, member(d))
+            send(wd.at[:, cols(d)], down.at[s, d], wsend_sem.at[2], wrecv_sem.at[2, d], s, member(d))
 
     pl.when(core == 0)(send_first_weights)
+
     own_gate = pltpu.make_async_copy(wg.at[cols(0), :], gate.at[s, 0], local_sem.at[0])
     own_up = pltpu.make_async_copy(wu.at[cols(0), :], up.at[s, 0], local_sem.at[1])
     own_down = pltpu.make_async_copy(wd.at[:, cols(0)], down.at[s, 0], local_sem.at[2])
@@ -160,12 +165,6 @@
         for d in (6, 2, 5, 7, 1, 3, 4):
             send(sssend.at[b], ssin.at[b, d], ssend_sem.at[b], srecv_sem.at[b], s, member(d))
 
-    arrived(xin, irecv_sem)
-    for h in range(2):
-        wide = xin[h].reshape(64, feat).astype(F32)
-        xcur[h] = wide
-        send_squares(h, 0, wide)
-
     def pass_on(tick):
         @pl.loop(0, chips)
         def _(i):
@@ -177,31 +176,30 @@
                 else:
                     hops = lax.rem(i - chip + chips, chips)
                     target = behind
-                cc = tick - 6 * i - hops
-
-                if way == 0:
-                    @pl.when((m == s) & (cc == 0))
-                    def _():
-                        own_gate.wait()
-                        own_up.wait()
-
-                        @pl.when(core == 1)
-                        def _():
-                            arrived(gate.at[s, pl.ds(1, 7)], wrecv_sem.at[0])
-                            arrived(up.at[s, pl.ds(1, 7)], wrecv_sem.at[1])
-
-                    @pl.when((m == s) & (cc == 4))
-                    def _():
-                        own_down.wait()
-                        arrived(down.at[s, pl.ds(1, 7)], wrecv_sem.at[2])
-
-                def move(ref, kind):
+                cc = tick - STRIDE * i - SKEW * hops
+
+                def move(array, kind, at, own_copy, own_at):
+                    ref = array.at[m, pl.ds(at, 2)]
                     sem = frecv_sem.at[m, 2 * cc + way]
 
                     @pl.when(hops > 0)
                     def _():
                         arrived(ref, sem)
 
+                    @pl.when(hops == 0)
+                    def _():
+                        if own_copy is None:
+                            arrived(array.at[m, at], wrecv_sem.at[kind, at])
+                        else:
+                            @pl.when(cc == own_at)
+                            def _():
+                                own_copy.wait()
+
+                            @pl.when(cc > own_at)
+                            def _():
+                                arrived(array.at[m, at], wrecv_sem.at[kind, at])
+                        arrived(array.at[m, at + 1], wrecv_sem.at[kind, at + 1])
+
                     @pl.when(hops < chips - 1)
                     def _():
                         send(ref, ref, fsend_sem.at[i, way, kind // 2], sem, target, e)
@@ -210,55 +208,49 @@
 
                 @pl.when((cc >= 0) & (cc < 4))
                 def _():
-                    move((gate, up)[way].at[m, pl.ds(2 * cc, 2)], way)
-
-                @pl.when((cc >= 4) & (cc < 6))
+                    move((gate, up)[way], way, 2 * cc, (own_gate, own_up)[way], 0)
+
+                @pl.when((cc >= 4) & (cc < PIECES))
                 def _():
-                    move(down.at[m, pl.ds(2 * cc - 8 + 4 * way, 2)], 2)
-
-    @pl.when(core == 0)
-    def _():
-        arrived(gate.at[s, pl.ds(1, 7)], wrecv_sem.at[0])
-        arrived(up.at[s, pl.ds(1, 7)], wrecv_sem.at[1])
-        send_last_weights()
-        pl.semaphore_signal(go_sem, inc=1, device_id=(mate, e), device_id_type=MESH)
-
-        @pl.loop(0, 9)
+                    move(down, 2, 2 * cc - 8 + 4 * way, own_down if way == 0 else None, 4)
+
+            @pl.when((core == 0) & (i == 0) & (tick == jnp.where(chip == 0, 3, 7)))
+            def _():
+                send_last_weights()
+                pl.semaphore_signal(go_sem, inc=1, device_id=(mate, e), device_id_type=MESH)
+
+    def pass_on_beside(m, step):
+        each = STRIDE // 2
+        low, high = (0, each // 3, 2 * each // 3, each)[step:step + 2]
+        third = FIRST // 3
+        first = jnp.where(m < core, third * step, FIRST + each * (m - core) + low)
+        last = jnp.where(m < core, third * (step + 1), FIRST + each * (m - core) + high)
+
+        @pl.loop(first, last)
         def _(tick):
             pass_on(tick)
 
-    @pl.when(core == 1)
-    def _():
-        pl.semaphore_wait(go_sem, 1)
-        send_first_weights()
-        send_last_weights()
-
-    def pass_on_beside(m, step):
-        @pl.when((core == 0) | (m > 0))
-        def _():
-            pass_on(9 + 3 * (m - core) + step)
-
-        @pl.when((core == 1) & (m == 0))
-        def _():
-            @pl.loop(3 * step, 3 * step + 3)
-            def _(tick):
-                pass_on(tick)
-
     def home_out(h, m):
+        b = slot(m, h)
+        scaled = (xcur[h] * allgain[m, pl.ds(j, 1), :]).astype(BF16)
+        ordered = jnp.dot(perm[m, h], scaled, preferred_element_type=F32).astype(BF16)
+        dsend[b] = ordered.reshape(4, 16, feat)
+        for d in (2, 1, 3):
+            send(dsend.at[b, d], drecv.at[b, d], dsend_sem.at[b], drecv_sem.at[b], s, other(d))
+        drecv[b, 0] = dsend[b, 0]
+
+    def scales_out(h, m):
         b = slot(m, h)
         arrived(ssin.at[b, pl.ds(1, 7)], srecv_sem.at[b])
         squares = ssin[b, 0]
         for d in range(1, GROUP):
             squares = squares + ssin[b, d]
-        row = jnp.broadcast_to(squares[0:1, 0:64], (64, 64))
-        col = jnp.sum(jnp.where(eye, row, 0.0), axis=1, keepdims=True)
-        scale = lax.rsqrt(col * (1.0 / width) + 1e-06)
-        normed = (xcur[h] * scale * allgain[m, pl.ds(j, 1), :]).astype(BF16)
-        ordered = jnp.dot(perm[m, h], normed, preferred_element_type=F32).astype(BF16)
-        dsend[b] = ordered.reshape(4, 16, feat)
+        row = lax.rsqrt(jnp.broadcast_to(squares[0:1, 0:64], (64, 64)) * (1.0 / width) + 1e-06)
+        col = jnp.sum(perm[m, h].astype(F32) * row, axis=1, keepdims=True)
+        scsend[b] = jnp.broadcast_to(col, (64, 128)).reshape(4, 16, 128)
         for d in (2, 1, 3):
-            send(dsend.at[b, d], drecv.at[b, d], dsend_sem.at[b], drecv_sem.at[b], s, other(d))
-        drecv[b, 0] = dsend[b, 0]
+            send(scsend.at[b, d], screcv.at[b, d], scsend_sem.at[b], screcv_sem.at[b], s, other(d))
+        screcv[b, 0] = scsend[b, 0]
 
     def first_products(h, m):
         b = slot(m, h)
@@ -288,13 +280,34 @@
 
     def hidden_units(h, m):
         b = slot(m, h)
+        arrived(screcv.at[b, pl.ds(1, 3)], screcv_sem.at[b])
         arrived(precv.at[b], precv_sem.at[b])
+        scale = screcv[b].reshape(64, 128)
         for half_at in range(2):
             both = own[b, half_at] + precv[b, half_at].astype(F32)
-            value = both[:, 0:128]
-            hbuf[b, 0, half_at] = (value / (1.0 + jnp.exp(-value)) * both[:, 128:256]).astype(BF16)
+            value = both[:, 0:128] * scale
+            hbuf[b, 0, half_at] = (value / (1.0 + jnp.exp(-value)) * (both[:, 128:256] * scale)).astype(BF16)
         for d in (2, 1, 3):
             send(hbuf.at[b, 0], hbuf.at[b, d], hsend_sem.at[b], hrecv_sem.at[b], s, row_member(d))
+
+    arrived(xin, irecv_sem)
+    for h in range(2):
+        wide = xin[h].reshape(64, feat).astype(F32)
+        xcur[h] = wide
+        home_out(h, 0)
+        send_squares(h, 0, wide)
+
+    @pl.when(core == 0)
+    def _():
+        @pl.loop(0, FIRST)
+        def _(tick):
+            pass_on(tick)
+
+    @pl.when(core == 1)
+    def _():
+        pl.semaphore_wait(go_sem, 1)
+        send_first_weights()
+        send_last_weights()
 
     def second_product(h, m):
         b = slot(m, h)
@@ -316,6 +329,7 @@
 
         @pl.when(m < n_pipe - 1)
         def _():
+            home_out(h, m + 1)
             send_squares(h, m + 1, wide)
 
         xsend[b] = fresh.reshape(4, 16, feat)
@@ -330,16 +344,19 @@
             def _():
                 send(xsend.at[b, q], obuf.at[m, :, cols(0)], xsend_sem.at[b], xrecv_sem.at[m], s, here + owner)
 
-    def hand_over(m):
+    def drain(m):
         for h in range(2):
             b = slot(m, h)
             arrived(dsend.at[b, pl.ds(1, 3)], dsend_sem.at[b])
             arrived(rsend.at[b], rsend_sem.at[b])
+            arrived(scsend.at[b, pl.ds(1, 3)], scsend_sem.at[b])
             arrived(psend.at[b], psend_sem.at[b])
             arrived(hbuf.at[b, pl.ds(1, 3)], hsend_sem.at[b])
             arrived(ysend.at[b, pl.ds(1, 3)], ysend_sem.at[b])
             arrived(ssin.at[b, pl.ds(1, 7)], ssend_sem.at[b])
             arrived(xsend.at[b], xsend_sem.at[b])
+
+    def hand_over(m):
         arrived(obuf.at[m, :, pl.ds(0, 7 * feat)], xrecv_sem.at[m])
 
         @pl.when(m == s)
@@ -352,9 +369,6 @@
 
     @pl.loop(0, n_pipe)
     def _(m):
-        for h in range(2):
-            home_out(h, m)
-
         pass_on_beside(m, 0)
 
         @pl.when(lax.rem(m, 2) != core)
@@ -364,15 +378,27 @@
 
         for h in range(2):
             first_products(h, m)
+        for h in range(2):
+            scales_out(h, m)
+
+        pass_on_beside(m, 1)
+
+        for h in range(2):
+            row_sums(h, m)
 
         @pl.when(m > 0)
         def _():
-            hand_over(m - 1)
-
-        for h in range(2):
-            row_sums(h, m)
-
-        pass_on_beside(m, 1)
+            drain(m - 1)
+
+        done = 2 * (m - n_pipe // 2)
+
+        @pl.when(done >= 0)
+        def _():
+            hand_over(done)
+
+        @pl.when((done >= 0) & (done + 1 < m))
+        def _():
+            hand_over(done + 1)
 
         for h in range(2):
             hidden_units(h, m)
@@ -389,6 +415,7 @@
         for h in range(2):
             home_in(h, m)
 
+    drain(n_pipe - 1)
     hand_over(n_pipe - 1)
 
     arrived(tabs.at[pl.ds(1, 7)], tsend_sem)
@@ -460,6 +487,8 @@
             pltpu.VMEM((n_pipe, 16, width), BF16),
             pltpu.VMEM((4, 8, 128), F32),
             pltpu.VMEM((4, GROUP, 8, 128), F32),
+            pltpu.VMEM((4, 4, 16, 128), F32),
+            pltpu.VMEM((4, 4, 16, 128), F32),
             pltpu.VMEM((4, 4, 16, feat), BF16),
             pltpu.VMEM((4, 4, 16, feat), BF16),
             pltpu.VMEM((4, 3, 2, 64, 256), BF16),
@@ -471,10 +500,10 @@
             pltpu.VMEM((4, 4, 16, feat), BF16),
             pltpu.VMEM((4, 4, 16, feat), BF16),
             pltpu.VMEM((4, 4, 16, feat), BF16),
-            dma((3,)), dma((3,)), dma((n_pipe // 2, 2, 2)), dma((n_pipe, 12)),
+            dma((3,)), dma((3, GROUP)), dma((n_pipe // 2, 2, 2)), dma((n_pipe, 2 * PIECES)),
             dma((n_pipe // 2, 3)), dma((n_pipe, 3)), dma, dma,
             dma, dma, dma, dma, dma, dma,
-            dma((4,)), dma((4,)), dma((4,)), dma((4,)), dma((4,)), dma((4,)), dma((4,)), dma((4,)),
+            dma((4,)), dma((4,)), dma((4,)), dma((4,)), dma((4,)), dma((4,)), dma((4,)), dma((4,)), dma((4,)), dma((4,)),
             dma((4,)), dma((4,)), dma((4,)), dma((4,)), dma((4,)), dma((n_pipe,)), dma((n_pipe,)), dma((n_pipe,)),
             dma((4,)), pltpu.SemaphoreType.REGULAR,
         ],

time: 427 us -> 415 us (0.972)
  Pallas kernels: 419 us -> 407 us
    pallas_call x1, Pallas kernels: 419 us -> 407 us  [local(): pl.pallas_call(functools.partial(kernel, n_pipe, width), out_shape=jax.Sh...]
where the time goes in v3:
time: 415 us
  Pallas kernels  407 us (98%)
  local copies, waits for them, and re-layouts  5.63 us (1%)
    pallas_call x1, Pallas kernels, local(): pl.pallas_call(functools.partial(kernel, n_pipe, width), out_shape=jax.Sh...  407 us

profile of v3, /device:TPU:39, one launch (start us, length us, event | category | flops | bytes accessed | tf_op | source)
XLA Modules:
  0.0 415.1 jit_solution(5715966158427509731)
XLA Ops:
  0.0 0.7 convert_element_type.14
  0.7 0.1 copy.10
  0.8 0.1 convert_element_type.15
  0.8 0.8 copy.11
  1.6 0.1 stack.6
  1.7 0.5 broadcast.5
  2.2 1.5 reduce.3
  3.6 0.6 reshape.27.gains
  4.3 0.7 tile.12.table
  4.9 407.3 %shard_map.73 = bf16[128,7168]{1,0:T(8,128)(2,1)} custom-call(bf16[128,7168]{1,0:T(8,128)(2,1)} %bitcast.14, bf16[7168,128]{1,0:T(8,128)(2,1)} %bitcast.15, bf16[7168,128]{1,0:T(8,128)(2,1)} %bitcast.16, bf16[128,7168]{1,0:T(8,128)(2,1)} %bitcast.17, f32[8,896]{1,0:T(8,128)} %reshape.27.gains, f32[2,8,128]{2,1,0:T(8,128)} %tile.12.table), custom_call_target="tpu_custom_call" | custom-call | tf_op jit(solution)/shard_map/pallas_call | solution.py:470
  412.3 2.8 copy.13
  (2 shorter events, 0.0 us)
